TPU v7x, 32 devices: a whole 2x2x4 slice. The times are simulated.
32 devices in a mesh: dp: 16 (over z, y, core), rep: 2 (over x).
Axes of the slice: x: 2, y: 2, z: 4, core: 2. Of those that a mesh axis runs over, the one named last changes fastest.
Arguments:
- passages: bfloat16 [2, 128, 128, 768], P(None, ('dp', 'rep')), may hold values from -6 to 6
- lengths: int32 [2, 128], P(None, ('dp', 'rep')), may hold values from 20 to 128, as said below
- queries: bfloat16 [2, 128, 768], P(None, ('dp', 'rep')), may hold values from -12 to 12
- positives: int32 [2, 128], P(None, ('dp', 'rep')), may hold values from 0 to 127
- out_grad: bfloat16 [2, 128, 128, 768], P(None, ('dp', 'rep')), may hold values from -6 to 6
- w_query: bfloat16 [768, 768], P('dp'), may hold values from -0.21875 to 0.21875
- b_query: bfloat16 [768], P('dp'), may hold values from -3 to 3
- w_key: bfloat16 [768, 768], P('dp'), may hold values from -0.21875 to 0.21875
- w_value: bfloat16 [768, 768], P('dp'), may hold values from -0.21875 to 0.21875
- b_value: bfloat16 [768], P('dp'), may hold values from -3 to 3
- w_out: bfloat16 [768, 768], P('dp'), may hold values from -0.625 to 0.625
- b_out: bfloat16 [768], P('dp'), may hold values from -3 to 3
- norm1_gain: bfloat16 [768], P('dp'), may hold values from 0.5 to 1.5
- norm1_bias: bfloat16 [768], P('dp'), may hold values from -3 to 3
- w_up: bfloat16 [768, 3072], P('dp'), may hold values from -0.21875 to 0.21875
- b_up: bfloat16 [3072], P('dp'), may hold values from -3 to 3
- w_down: bfloat16 [3072, 768], P('dp'), may hold values from -0.109375 to 0.109375
- b_down: bfloat16 [768], P('dp'), may hold values from -3 to 3
- norm2_gain: bfloat16 [768], P('dp'), may hold values from 0.5 to 1.5
- norm2_bias: bfloat16 [768], P('dp'), may hold values from -3 to 3
Outputs:
- output: bfloat16 [2, 128, 128, 768], P(None, ('dp', 'rep'))
- query_loss: float32 [2, 128], P(None, ('dp', 'rep'))
- passages_grad: float32 [2, 128, 128, 768], P(None, ('dp', 'rep'))
- queries_grad: float32 [2, 128, 768], P(None, ('dp', 'rep'))
- passage_cls_grad: float32 [2, 128, 768], P(None, ('dp', 'rep'))
- grad_w_query: float32 [768, 768], P('dp')
- grad_b_query: float32 [768], P('dp')
- grad_w_key: float32 [768, 768], P('dp')
- grad_w_value: float32 [768, 768], P('dp')
- grad_b_value: float32 [768], P('dp')
- grad_w_out: float32 [768, 768], P('dp')
- grad_b_out: float32 [768], P('dp')
- grad_norm1_gain: float32 [768], P('dp')
- grad_norm1_bias: float32 [768], P('dp')
- grad_w_up: float32 [768, 3072], P('dp')
- grad_b_up: float32 [3072], P('dp')
- grad_w_down: float32 [3072, 768], P('dp')
- grad_b_down: float32 [768], P('dp')
- grad_norm2_gain: float32 [768], P('dp')
- grad_norm2_bias: float32 [768], P('dp')
Inputs may be any that keep to these rules, and one draw needn't show every extreme that they name: `lengths`: in every micro-batch some passage has length 128 and some has 20.
All inputs are finite; a program needn't handle non-finite values.
Results may differ from a plain program's by a relative error of at most 0.014.
Values may be sent and summed in bfloat16 or wider, within the bound.
No kernel may reach another device: no remote copies, remote signals or barrier semaphores. Data moves between devices by JAX's collectives and lax.ppermute only.
A program may use at most 192 MiB of HBM per device.

v0:
```python
import math

import jax
import jax.numpy as jnp
from jax import lax
from jax.sharding import PartitionSpec as P

H = 12


HIGH = lax.Precision.HIGHEST


def layer_norm(v, gain, bias):
    mean_val = jnp.mean(v, axis=-1, keepdims=True)
    centred = v - mean_val
    variance = jnp.mean(centred * centred, axis=-1, keepdims=True)
    return centred * lax.rsqrt(variance + 1e-05) * gain + bias


def gelu_exact(v):
    return jax.nn.gelu(v, approximate=False)


def scores_of(query_heads, key_heads, key_valid, score_scale):
    raw_scores = (
        jnp.einsum("plhe,pmhe->phlm", query_heads, key_heads, preferred_element_type=jnp.float32)
        * score_scale
    )
    return jnp.where(key_valid, raw_scores, -1000000000.0)


def project(left, right):
    return jnp.dot(left, right, preferred_element_type=jnp.float32)


def project_left(left, right):
    return jnp.einsum("rd,re->de", left, right, preferred_element_type=jnp.float32)


def project_back(left, right):
    return jnp.einsum("re,de->rd", left, right, preferred_element_type=jnp.float32)


def row_total(values):
    return jnp.sum(values.astype(jnp.float32), axis=0)


def per_device(
    passages,
    lengths,
    queries,
    positives,
    out_grad,
    w_query,
    b_query,
    w_key,
    w_value,
    b_value,
    w_out,
    b_out,
    norm1_gain,
    norm1_bias,
    w_up,
    b_up,
    w_down,
    b_down,
    norm2_gain,
    norm2_bias,
):
    steps_count, passage_count, length, model_width = passages.shape
    head_width = model_width // H
    rows_count = passage_count * length
    head_shape = (passage_count, length, H, head_width)
    score_scale = 1.0 / math.sqrt(head_width)
    inv_width = 1.0 / math.sqrt(model_width)
    outputs = []
    losses = []
    input_grads = []
    query_grads = []
    cls_grads_all = []
    totals = None
    for micro_step in range(steps_count):
        gathered = (
            lax.all_gather(w_query, "dp", axis=0, tiled=True),
            lax.all_gather(b_query, "dp", axis=0, tiled=True),
            lax.all_gather(w_key, "dp", axis=0, tiled=True),
            lax.all_gather(w_value, "dp", axis=0, tiled=True),
            lax.all_gather(b_value, "dp", axis=0, tiled=True),
            lax.all_gather(w_out, "dp", axis=0, tiled=True),
            lax.all_gather(b_out, "dp", axis=0, tiled=True),
            lax.all_gather(norm1_gain, "dp", axis=0, tiled=True),
            lax.all_gather(norm1_bias, "dp", axis=0, tiled=True),
            lax.all_gather(w_up, "dp", axis=0, tiled=True),
            lax.all_gather(b_up, "dp", axis=0, tiled=True),
            lax.all_gather(w_down, "dp", axis=0, tiled=True),
            lax.all_gather(b_down, "dp", axis=0, tiled=True),
            lax.all_gather(norm2_gain, "dp", axis=0, tiled=True),
            lax.all_gather(norm2_bias, "dp", axis=0, tiled=True),
        )
        (
            weight_query,
            bias_query,
            weight_key,
            weight_value,
            bias_value,
            weight_out,
            bias_out,
            gain_one,
            shift_one,
            weight_up,
            bias_up,
            weight_down,
            bias_down,
            gain_two,
            shift_two,
        ) = gathered
        token_rows = passages[micro_step].reshape(rows_count, model_width)
        key_valid = (jnp.arange(length)[None, :] < lengths[micro_step][:, None])[:, None, None, :]
        query_rows = (project(token_rows, weight_query) + bias_query.astype(jnp.float32)).astype(
            jnp.bfloat16
        )
        key_rows = project(token_rows, weight_key).astype(jnp.bfloat16)
        value_rows = (project(token_rows, weight_value) + bias_value.astype(jnp.float32)).astype(
            jnp.bfloat16
        )
        query_heads = query_rows.reshape(head_shape)
        key_heads = key_rows.reshape(head_shape)
        value_heads = value_rows.reshape(head_shape)
        scores = scores_of(query_heads, key_heads, key_valid, score_scale)
        log_total = jax.nn.logsumexp(scores, axis=-1, keepdims=True)
        probs_low = jnp.exp(scores - log_total).astype(jnp.bfloat16)
        context = jnp.einsum(
            "phlm,pmhe->plhe", probs_low, value_heads, preferred_element_type=jnp.float32
        )
        context = context.astype(jnp.bfloat16).reshape(rows_count, model_width)
        gain_one_f = gain_one.astype(jnp.float32)
        shift_one_f = shift_one.astype(jnp.float32)
        gain_two_f = gain_two.astype(jnp.float32)
        shift_two_f = shift_two.astype(jnp.float32)
        sum_one = (
            token_rows.astype(jnp.float32)
            + project(context, weight_out)
            + bias_out.astype(jnp.float32)
        )
        hidden_one = layer_norm(sum_one, gain_one_f, shift_one_f)
        hidden_low = hidden_one.astype(jnp.bfloat16)
        hidden_pre = project(hidden_low, weight_up) + bias_up.astype(jnp.float32)
        gelu_low = gelu_exact(hidden_pre).astype(jnp.bfloat16)
        sum_two = hidden_one + project(gelu_low, weight_down) + bias_down.astype(jnp.float32)
        result, pull_two = jax.vjp(layer_norm, sum_two, gain_two_f, shift_two_f)
        result = result.reshape(passage_count, length, model_width)
        outputs.append(result.astype(jnp.bfloat16))
        cls_all = lax.all_gather(
            result[:, 0, :].astype(jnp.bfloat16), ("dp", "rep"), axis=0, tiled=True
        )
        queries_now = queries[micro_step]
        logits = (
            jnp.einsum("qd,pd->qp", queries_now, cls_all, preferred_element_type=jnp.float32)
            * inv_width
        )
        query_total = jax.nn.logsumexp(logits, axis=-1)
        onehot = (positives[micro_step][:, None] == jnp.arange(cls_all.shape[0])[None, :]).astype(
            jnp.float32
        )
        losses.append(query_total - jnp.sum(logits * onehot, axis=-1))
        logit_grad = (jnp.exp(logits - query_total[:, None]) - onehot) * inv_width
        query_grads.append(jnp.dot(logit_grad, cls_all.astype(jnp.float32), precision=HIGH))
        cls_partial = jnp.einsum(
            "qp,qd->pd", logit_grad, queries_now.astype(jnp.float32), precision=HIGH
        )
        cls_grad = lax.psum_scatter(cls_partial, ("dp", "rep"), scatter_dimension=0, tiled=True)
        cls_grads_all.append(cls_grad)
        gathered = (
            lax.all_gather(w_query, "dp", axis=0, tiled=True),
            lax.all_gather(b_query, "dp", axis=0, tiled=True),
            lax.all_gather(w_key, "dp", axis=0, tiled=True),
            lax.all_gather(w_value, "dp", axis=0, tiled=True),
            lax.all_gather(b_value, "dp", axis=0, tiled=True),
            lax.all_gather(w_out, "dp", axis=0, tiled=True),
            lax.all_gather(b_out, "dp", axis=0, tiled=True),
            lax.all_gather(norm1_gain, "dp", axis=0, tiled=True),
            lax.all_gather(norm1_bias, "dp", axis=0, tiled=True),
            lax.all_gather(w_up, "dp", axis=0, tiled=True),
            lax.all_gather(b_up, "dp", axis=0, tiled=True),
            lax.all_gather(w_down, "dp", axis=0, tiled=True),
            lax.all_gather(b_down, "dp", axis=0, tiled=True),
            lax.all_gather(norm2_gain, "dp", axis=0, tiled=True),
            lax.all_gather(norm2_bias, "dp", axis=0, tiled=True),
        )
        (
            weight_query,
            bias_query,
            weight_key,
            weight_value,
            bias_value,
            weight_out,
            bias_out,
            gain_one,
            shift_one,
            weight_up,
            bias_up,
            weight_down,
            bias_down,
            gain_two,
            shift_two,
        ) = gathered
        grad_output = out_grad[micro_step].astype(jnp.float32).at[:, 0, :].add(cls_grad)
        grad_sum_two, grad_gain_two, grad_shift_two = pull_two(
            grad_output.reshape(rows_count, model_width)
        )
        branch_low = grad_sum_two.astype(jnp.bfloat16)
        grad_b_down = row_total(branch_low)
        grad_w_down = project_left(gelu_low, branch_low)
        _, pull_gelu = jax.vjp(gelu_exact, hidden_pre)
        up_low = pull_gelu(project_back(branch_low, weight_down))[0].astype(jnp.bfloat16)
        grad_b_up = row_total(up_low)
        grad_w_up = project_left(hidden_low, up_low)
        grad_hidden = grad_sum_two + project_back(up_low, weight_up)
        _, pull_one = jax.vjp(layer_norm, sum_one, gain_one_f, shift_one_f)
        grad_sum_one, grad_gain_one, grad_shift_one = pull_one(grad_hidden)
        attn_low = grad_sum_one.astype(jnp.bfloat16)
        grad_b_out = row_total(attn_low)
        grad_w_out = project_left(context, attn_low)
        context_grad = project_back(attn_low, weight_out).astype(jnp.bfloat16).reshape(head_shape)
        scores = scores_of(query_heads, key_heads, key_valid, score_scale)
        attn_probs = jnp.exp(scores - log_total)
        probs_grad = jnp.einsum(
            "plhe,pmhe->phlm", context_grad, value_heads, preferred_element_type=jnp.float32
        )
        score_grad = attn_probs * (
            probs_grad - jnp.sum(probs_grad * attn_probs, axis=-1, keepdims=True)
        )
        score_low = score_grad.astype(jnp.bfloat16)
        query_low = (
            (
                jnp.einsum(
                    "phlm,pmhe->plhe", score_low, key_heads, preferred_element_type=jnp.float32
                )
                * score_scale
            )
            .astype(jnp.bfloat16)
            .reshape(rows_count, model_width)
        )
        key_low = (
            (
                jnp.einsum(
                    "phlm,plhe->pmhe", score_low, query_heads, preferred_element_type=jnp.float32
                )
                * score_scale
            )
            .astype(jnp.bfloat16)
            .reshape(rows_count, model_width)
        )
        value_low = (
            jnp.einsum(
                "phlm,plhe->pmhe", probs_low, context_grad, preferred_element_type=jnp.float32
            )
            .astype(jnp.bfloat16)
            .reshape(rows_count, model_width)
        )
        grad_w_query = project_left(token_rows, query_low)
        grad_b_query = row_total(query_low)
        grad_w_key = project_left(token_rows, key_low)
        grad_w_value = project_left(token_rows, value_low)
        grad_b_value = row_total(value_low)
        input_grad = (
            grad_sum_one
            + project_back(query_low, weight_query)
            + project_back(key_low, weight_key)
            + project_back(value_low, weight_value)
        )
        input_grads.append(input_grad.reshape(passage_count, length, model_width))
        micro_grads = (
            grad_w_query,
            grad_b_query,
            grad_w_key,
            grad_w_value,
            grad_b_value,
            grad_w_out,
            grad_b_out,
            grad_gain_one,
            grad_shift_one,
            grad_w_up,
            grad_b_up,
            grad_w_down,
            grad_b_down,
            grad_gain_two,
            grad_shift_two,
        )
        if totals is None:
            totals = micro_grads
        else:
            totals = tuple((left + right for left, right in zip(totals, micro_grads)))
    (
        total_w_query,
        total_b_query,
        total_w_key,
        total_w_value,
        total_b_value,
        total_w_out,
        total_b_out,
        total_gain_one,
        total_shift_one,
        total_w_up,
        total_b_up,
        total_w_down,
        total_b_down,
        total_gain_two,
        total_shift_two,
    ) = totals
    shard_grads = (
        lax.psum_scatter(total_w_query, "dp", scatter_dimension=0, tiled=True),
        lax.psum_scatter(total_b_query, "dp", scatter_dimension=0, tiled=True),
        lax.psum_scatter(total_w_key, "dp", scatter_dimension=0, tiled=True),
        lax.psum_scatter(total_w_value, "dp", scatter_dimension=0, tiled=True),
        lax.psum_scatter(total_b_value, "dp", scatter_dimension=0, tiled=True),
        lax.psum_scatter(total_w_out, "dp", scatter_dimension=0, tiled=True),
        lax.psum_scatter(total_b_out, "dp", scatter_dimension=0, tiled=True),
        lax.psum_scatter(total_gain_one, "dp", scatter_dimension=0, tiled=True),
        lax.psum_scatter(total_shift_one, "dp", scatter_dimension=0, tiled=True),
        lax.psum_scatter(total_w_up, "dp", scatter_dimension=0, tiled=True),
        lax.psum_scatter(total_b_up, "dp", scatter_dimension=0, tiled=True),
        lax.psum_scatter(total_w_down, "dp", scatter_dimension=0, tiled=True),
        lax.psum_scatter(total_b_down, "dp", scatter_dimension=0, tiled=True),
        lax.psum_scatter(total_gain_two, "dp", scatter_dimension=0, tiled=True),
        lax.psum_scatter(total_shift_two, "dp", scatter_dimension=0, tiled=True),
    )
    (
        shard_w_query,
        shard_b_query,
        shard_w_key,
        shard_w_value,
        shard_b_value,
        shard_w_out,
        shard_b_out,
        shard_gain_one,
        shard_shift_one,
        shard_w_up,
        shard_b_up,
        shard_w_down,
        shard_b_down,
        shard_gain_two,
        shard_shift_two,
    ) = shard_grads
    final_grads = lax.psum(
        (
            shard_w_query,
            shard_b_query,
            shard_w_key,
            shard_w_value,
            shard_b_value,
            shard_w_out,
            shard_b_out,
            shard_gain_one,
            shard_shift_one,
            shard_w_up,
            shard_b_up,
            shard_w_down,
            shard_b_down,
            shard_gain_two,
            shard_shift_two,
        ),
        "rep",
    )
    (
        final_w_query,
        final_b_query,
        final_w_key,
        final_w_value,
        final_b_value,
        final_w_out,
        final_b_out,
        final_gain_one,
        final_shift_one,
        final_w_up,
        final_b_up,
        final_w_down,
        final_b_down,
        final_gain_two,
        final_shift_two,
    ) = final_grads
    return (
        jnp.stack(outputs),
        jnp.stack(losses),
        jnp.stack(input_grads),
        jnp.stack(query_grads),
        jnp.stack(cls_grads_all),
        final_w_query,
        final_b_query,
        final_w_key,
        final_w_value,
        final_b_value,
        final_w_out,
        final_b_out,
        final_gain_one,
        final_shift_one,
        final_w_up,
        final_b_up,
        final_w_down,
        final_b_down,
        final_gain_two,
        final_shift_two,
    )


def solution(mesh):
    return jax.shard_map(
        per_device,
        mesh=mesh,
        in_specs=(
            P(None, ("dp", "rep"), None, None),
            P(None, ("dp", "rep")),
            P(None, ("dp", "rep"), None),
            P(None, ("dp", "rep")),
            P(None, ("dp", "rep"), None, None),
            P("dp", None),
            P("dp"),
            P("dp", None),
            P("dp", None),
            P("dp"),
            P("dp", None),
            P("dp"),
            P("dp"),
            P("dp"),
            P("dp", None),
            P("dp"),
            P("dp", None),
            P("dp"),
            P("dp"),
            P("dp"),
        ),
        out_specs=(
            P(None, ("dp", "rep"), None, None),
            P(None, ("dp", "rep")),
            P(None, ("dp", "rep"), None, None),
            P(None, ("dp", "rep"), None),
            P(None, ("dp", "rep"), None),
            P("dp", None),
            P("dp"),
            P("dp", None),
            P("dp", None),
            P("dp"),
            P("dp", None),
            P("dp"),
            P("dp"),
            P("dp"),
            P("dp", None),
            P("dp"),
            P("dp", None),
            P("dp"),
            P("dp"),
            P("dp"),
        ),
        check_vma=False,
    )
```

profile of v0, /device:TPU:0, one launch (start us, length us, event | category | flops | bytes accessed | tf_op | source)
XLA Modules:
  0.0 1217.8 jit_solution(16629880033291223454)
XLA Ops:
  23.4 63.5 %all-reduce.24 = (bf16[768]{0:T(1024)(128)(2,1)S(1)}, bf16[768]{0:T(1024)(128)(2,1)S(1)}, bf16[768]{0:T(1024)(128)(2,1)S(1)}, bf16[768]{0:T(1024)(128)(2,1)S(1)}...) all-reduce(bf16[768]{0:T(1024)(128)(2,1)S(1)} %dynamic-update-slice, ...), channel_id=1, replica_groups=mesh['dp'=16,'rep'=2] {'dp'}, use_global_device_ids=true, to_apply=%add.2 | all-reduce | flops 9216 | bytes 36864
  101.8 29.1 %all-gather.9.cloned.1.call-done = bf16[768,768]{1,0:T(8,128)(2,1)} async-done(((bf16[48,768]{1,0:T(8,128)(2,1)}), bf16[768,768]{1,0:T(8,128)(2,1)}) %all-gather.9.cloned.1.call-update) | async-done | bytes 1179664 | tf_op jit(solution)/shard_map/all_gather | solution.py:88
  150.1 20.2 %all-gather.15.cloned.1.call-done = bf16[768,768]{1,0:T(8,128)(2,1)} async-done(((bf16[48,768]{1,0:T(8,128)(2,1)}), bf16[768,768]{1,0:T(8,128)(2,1)}) %all-gather.15.cloned.1.call-update) | async-done | bytes 1179664 | tf_op jit(solution)/shard_map/all_gather | solution.py:90
  179.9 44.9 %all-gather.17.cloned.1.call-done = bf16[768,3072]{1,0:T(8,128)(2,1)} async-done(((bf16[48,3072]{1,0:T(8,128)(2,1)}), bf16[768,3072]{1,0:T(8,128)(2,1)}) %all-gather.17.cloned.1.call-update) | async-done | bytes 4718608 | tf_op jit(solution)/shard_map/all_gather | solution.py:94
  224.8 4.8 fusion.149
  232.4 34.8 %multiply_convert_fusion.1 = (bf16[512,3072]{1,0:T(8,128)(2,1)}, f32[512,3072]{1,0:T(8,128)}, bf16[512,3072]{1,0:T(8,128)(2,1)}, f32[512,3072]{1,0:T(8,128)}, f32[512,3072]{1,0:T(8,128)}) fusion(f32[3072]{0:T(1024)S(1)} %copy-done.120, f32[512,3072]{1,0:T(8,128)S(1)} %fusion.149, bf16[768,3072]{1,0:T(8,128)(2,1)S(1)} %copy-done.163, ...), kind=kOutput, calls=%fused_computation.21 | convolution fusion | flops 2625503232 | bytes 37771264 | tf_op jit(solution)/shard_map/dot_general | solution.py:34
  267.2 11.7 all-gather.19.cloned.1.call-done
  278.9 6.6 fusion.166
  290.9 68.1 %all-gather = bf16[128,1,768]{2,1,0:T(2,128)(2,1)S(1)} all-gather(bf16[4,1,768]{2,1,0:T(2,128)(2,1)S(1)} %slice.96), channel_id=2, replica_groups=mesh['dp'=16,'rep'=2] {'dp','rep'}, dimensions={0}, use_global_device_ids=true | all-gather | bytes 202752 | tf_op jit(solution)/shard_map/all_gather | solution.py:154
  360.6 65.4 %all-gather.1 = bf16[128,1,768]{2,1,0:T(2,128)(2,1)S(1)} all-gather(bf16[4,1,768]{2,1,0:T(2,128)(2,1)S(1)} %slice.97), channel_id=3, replica_groups=mesh['dp'=16,'rep'=2] {'dp','rep'}, dimensions={0}, use_global_device_ids=true | all-gather | bytes 202752 | tf_op jit(solution)/shard_map/all_gather | solution.py:154
  437.2 120.7 %all-reduce.28.cloned.1.call-done = (f32[128,768]{1,0:T(8,128)}, f32[128,768]{1,0:T(8,128)}) async-done(((f32[128,768]{1,0:T(8,128)}, f32[128,768]{1,0:T(8,128)}), (f32[128,768]{1,0:T(8,128)}, f32[128,768]{1,0:T(8,128)})) %all-reduce.28.cloned.1.call-update) | async-done | bytes 786448
  573.6 17.9 %convert_reduce_fusion.1 = (f32[3072]{0:T(1024)}, bf16[512,3072]{1,0:T(8,128)(2,1)}, f32[3072]{0:T(1024)}, bf16[512,3072]{1,0:T(8,128)(2,1)}) fusion(f32[512,3072]{1,0:T(8,128)} %get-tuple-element.174, f32[512,3072]{1,0:T(8,128)} %get-tuple-element.210, f32[3072]{0:T(1024)S(1)} %copy-done.121, f32[512,3072]{1,0:T(8,128)} %fusion.170, ...), kind=kOutput, calls=%fused_computation.5 | convolution fusion | flops 2469390336 | bytes 43290624 | tf_op jit(solution)/shard_map/re,de->rd/dot_general | solution.py:42
  591.5 6.1 add_add_fusion.10
  597.7 6.4 multiply_reduce_fusion.3
  670.2 5.4 convolution_add_fusion
  677.0 5.0 fusion.151
  682.0 5.7 convolution_add_fusion.1
  700.2 60.7 %reduce-scatter.19.cloned.1.call-done = f32[48,768]{1,0:T(8,128)} async-done(((f32[768,768]{1,0:T(8,128)}), f32[48,768]{1,0:T(8,128)}) %reduce-scatter.19.cloned.1.call-update) | async-done | bytes 147472
  762.7 64.2 %reduce-scatter.21.cloned.1.call-done = f32[48,768]{1,0:T(8,128)} async-done(((f32[768,768]{1,0:T(8,128)}), f32[48,768]{1,0:T(8,128)}) %reduce-scatter.21.cloned.1.call-update) | async-done | bytes 147472
  828.7 63.9 %reduce-scatter.13.cloned.1.call-done = f32[48,768]{1,0:T(8,128)} async-done(((f32[768,768]{1,0:T(8,128)}), f32[48,768]{1,0:T(8,128)}) %reduce-scatter.13.cloned.1.call-update) | async-done | bytes 147472 | tf_op jit(solution)/shard_map/reduce_scatter | solution.py:318
  892.7 114.9 %reduce-scatter.17.cloned.1.call-done = f32[192,768]{1,0:T(8,128)} async-done(((f32[3072,768]{1,0:T(8,128)}), f32[192,768]{1,0:T(8,128)}) %reduce-scatter.17.cloned.1.call-update) | async-done | bytes 589840 | tf_op jit(solution)/shard_map/reduce_scatter | solution.py:324
  1007.6 115.2 %reduce-scatter.15.cloned.1.call-done = f32[48,3072]{1,0:T(8,128)} async-done(((f32[768,3072]{1,0:T(8,128)}), f32[48,3072]{1,0:T(8,128)}) %reduce-scatter.15.cloned.1.call-update) | async-done | bytes 589840 | tf_op jit(solution)/shard_map/reduce_scatter | solution.py:322
  1124.6 60.8 %all-reduce.21 = (f32[768]{0:T(1024)S(1)}, f32[768]{0:T(1024)S(1)}, f32[768]{0:T(1024)S(1)}, f32[768]{0:T(1024)S(1)}, f32[768]{0:T(1024)S(1)}, /*index=5*/f32[30...) all-reduce(f32[768]{0:T(1024)S(1)} %add.410, ...), channel_id=7, replica_groups=mesh['dp'=16,'rep'=2] {'dp'}, use_global_device_ids=true, to_apply=%region_34.35.clone | all-reduce | flops 9216 | bytes 73728
  1186.0 5.7 all-reduce.22
  (575 shorter events, 196.8 us)
Async XLA Ops:
  7.2 84.3 %all-gather.13.cloned.1.call-start = ((), (), s32[]{:S(2)}) async-start(), calls=%async_computation.8 | async-start | bytes 1253376 | tf_op jit(solution)/shard_map/all_gather | solution.py:87
  7.9 87.0 %all-gather.11.cloned.1.call-start = ((), (), s32[]{:S(2)}) async-start(), calls=%async_computation.7 | async-start | bytes 1253376 | tf_op jit(solution)/shard_map/all_gather | solution.py:85
  8.7 122.2 %all-gather.9.cloned.1.call-start = ((), (), s32[]{:S(2)}) async-start(), calls=%async_computation.6 | async-start | bytes 1253376 | tf_op jit(solution)/shard_map/all_gather | solution.py:88
  9.4 160.9 %all-gather.15.cloned.1.call-start = ((), (), s32[]{:S(2)}) async-start(), calls=%async_computation.9 | async-start | bytes 1253376 | tf_op jit(solution)/shard_map/all_gather | solution.py:90
  10.0 214.8 %all-gather.17.cloned.1.call-start = ((), (), s32[]{:S(2)}) async-start(), calls=%async_computation.10 | async-start | bytes 5013504 | tf_op jit(solution)/shard_map/all_gather | solution.py:94
  10.6 268.3 %all-gather.19.cloned.1.call-start = ((), (), s32[]{:S(2)}) async-start(), calls=%async_computation.11 | async-start | bytes 5013504 | tf_op jit(solution)/shard_map/all_gather | solution.py:96
  11.1 546.7 %all-reduce.28.cloned.1.call-start = ((), (), s32[]{:S(2)}) async-start(), calls=%async_computation.18 | async-start | bytes 1572864
  90.8 79.5 %copy-start.25 = (bf16[1,4,128,768]{3,2,1,0:T(8,128)(2,1)}, bf16[1,4,128,768]{3,2,1,0:T(8,128)(2,1)S(1)}, u32[]{:S(2)}) copy-start(bf16[1,4,128,768]{3,2,1,0:T(8,128)(2,1)S(1)} %get-tuple-element.179) | copy-start | bytes 2359300
  90.8 87.8 %copy-start.21 = (bf16[1,4,128,768]{3,2,1,0:T(8,128)(2,1)}, bf16[1,4,128,768]{3,2,1,0:T(8,128)(2,1)S(1)}, u32[]{:S(2)}) copy-start(bf16[1,4,128,768]{3,2,1,0:T(8,128)(2,1)S(1)} %get-tuple-element.180) | copy-start | bytes 2359300
  172.7 106.2 %copy-start.100 = (f32[512]{0:T(512)}, f32[512]{0:T(512)S(1)}, u32[]{:S(2)}) copy-start(f32[512]{0:T(512)S(1)} %broadcast_multiply_fusion.3) | copy-start | bytes 6148
  173.8 105.1 %copy-start.125 = (f32[512]{0:T(512)}, f32[512]{0:T(512)S(1)}, u32[]{:S(2)}) copy-start(f32[512]{0:T(512)S(1)} %fusion.126) | copy-start | bytes 6148
  179.9 106.0 %copy-start.92 = (f32[512]{0:T(512)}, f32[512]{0:T(512)S(1)}, u32[]{:S(2)}) copy-start(f32[512]{0:T(512)S(1)} %fusion.128) | copy-start | bytes 6148
  289.2 70.2 %copy-start.140 = (s32[4]{0:T(128)S(1)}, s32[4]{0:T(128)}, u32[]{:S(2)}) copy-start(s32[4]{0:T(128)} %get-tuple-element.196) | copy-start | bytes 52
  289.2 137.9 %copy-start.138 = (s32[4]{0:T(128)S(1)}, s32[4]{0:T(128)}, u32[]{:S(2)}) copy-start(s32[4]{0:T(128)} %get-tuple-element.197) | copy-start | bytes 52
  430.2 268.0 %reduce-scatter.23.cloned.1.call-start = ((), (), s32[]{:S(2)}) async-start(), calls=%async_computation.17 | async-start | bytes 2506752
  633.0 127.8 %reduce-scatter.19.cloned.1.call-start = ((), (), s32[]{:S(2)}) async-start(), calls=%async_computation.15 | async-start | bytes 2506752
  649.3 177.6 %reduce-scatter.21.cloned.1.call-start = ((), (), s32[]{:S(2)}) async-start(), calls=%async_computation.16 | async-start | bytes 2506752
  659.8 232.8 %reduce-scatter.13.cloned.1.call-start = ((), (), s32[]{:S(2)}) async-start(), calls=%async_computation.12 | async-start | bytes 2506752 | tf_op jit(solution)/shard_map/reduce_scatter | solution.py:318
  664.3 343.3 %reduce-scatter.17.cloned.1.call-start = ((), (), s32[]{:S(2)}) async-start(), calls=%async_computation.14 | async-start | bytes 10027008 | tf_op jit(solution)/shard_map/reduce_scatter | solution.py:324
  675.6 447.2 %reduce-scatter.15.cloned.1.call-start = ((), (), s32[]{:S(2)}) async-start(), calls=%async_computation.13 | async-start | bytes 10027008 | tf_op jit(solution)/shard_map/reduce_scatter | solution.py:322
  687.9 513.3 %all-reduce.30.cloned.1.call-start = ((), (), s32[]{:S(2)}) async-start(), calls=%async_computation.19 | async-start | bytes 5013504 | tf_op jit(solution)/shard_map/psum | solution.py:346
  698.2 425.4 %copy-start.12 = (f32[4,128,768]{2,0,1:T(4,128)S(1)}, f32[4,128,768]{2,0,1:T(4,128)}, u32[]{:S(2)}) copy-start(f32[4,128,768]{2,0,1:T(4,128)} %fusion.103) | copy-start | bytes 4718596
  762.7 361.2 %copy-start.11 = (f32[4,128,768]{2,0,1:T(4,128)S(1)}, f32[4,128,768]{2,0,1:T(4,128)}, u32[]{:S(2)}) copy-start(f32[4,128,768]{2,0,1:T(4,128)} %copy-done.10) | copy-start | bytes 4718596
  1124.2 70.0 %copy-start.65 = (bf16[4,128,12,64]{1,0,3,2:T(4,128)(2,1)S(1)}, bf16[4,128,12,64]{1,0,3,2:T(4,128)(2,1)}, u32[]{:S(2)}) copy-start(bf16[4,128,12,64]{1,0,3,2:T(4,128)(2,1)} %copy-done.64) | copy-start | bytes 2359300
  (164 other events, 993.4 us)
Sparse Core Ops, SparseCore 0:
  10.3 41.1 all-gather.12
  53.7 37.4 all-gather.10
  93.5 37.3 all-gather.8
  133.0 37.2 all-gather.14
  172.5 52.3 all-gather.16
  226.9 51.9 all-gather.18
  430.3 127.5 all-reduce.27
  633.2 61.9 reduce-scatter.22
  698.9 61.9 reduce-scatter.18
  765.0 61.8 reduce-scatter.20
  830.7 61.9 reduce-scatter.12
  897.2 110.3 reduce-scatter.16
  1011.7 111.0 reduce-scatter.14
  1126.7 72.6 all-reduce.29
where the time goes:
time: 1220 us
  waiting for transfers between devices  649 us (53%)
  blocking collectives  263 us (22%)
  matrix products  170 us (14%)
  local copies, waits for them, and re-layouts  82.4 us (7%)
  other arithmetic  32.6 us (3%)
  between operations  19.3 us (2%)
    unnamed x18, waiting for transfers between devices  249 us
    all_gather x2, blocking collectives, per_device(): lax.all_gather(result[:, 0, :].astype(jnp.bfloat16), ('dp', 'rep'), axis=...  133 us
    unnamed x2, blocking collectives  124 us
    reduce_scatter x1, waiting for transfers between devices, per_device(): lax.psum_scatter(total_w_up, 'dp', scatter_dimension=0, tiled=True)  115 us
    reduce_scatter x1, waiting for transfers between devices, per_device(): lax.psum_scatter(total_w_down, 'dp', scatter_dimension=0, tiled=True)  115 us
    dot_general x12, matrix products, project(): return jnp.dot(left, right, preferred_element_type=jnp.float32)  65.8 us
    reduce_scatter x1, waiting for transfers between devices, per_device(): lax.psum_scatter(total_w_out, 'dp', scatter_dimension=0, tiled=True)  63.9 us
    unnamed x388, local copies, waits for them, and re-layouts  50.9 us
  transfers between devices with their start and end apart: 14, of which 10 were waited for; matrix products, arithmetic and copies ran while one was open for 14% of the time, Pallas kernels for 0%

commit v1 on v0

v1 whole, which is shorter than its diff:
```python
import functools
import math

import jax
import jax.numpy as jnp
from jax import lax
from jax.sharding import PartitionSpec as P

H = 12
F32 = jnp.float32
BF16 = jnp.bfloat16
INV_SQRT2 = 1.0 / math.sqrt(2.0)
INV_SQRT_2PI = 1.0 / math.sqrt(2.0 * math.pi)


class Grid:
    def __init__(self, dp, rep):
        self.dp, self.rep = dp, rep
        self.core = 2 if dp % 2 == 0 else 1
        rest = dp // self.core
        self.z = 4 if rest % 4 == 0 else 1
        self.y = rest // self.z
        self.stride = {"core": 1, "y": self.core, "z": self.core * self.y}
        self.size = {"core": self.core, "y": self.y, "z": self.z, "rep": rep}

    def positions(self):
        dp_index = lax.axis_index("dp")
        pos = {
            name: (dp_index // self.stride[name]) % self.size[name] for name in ("core", "y", "z")
        }
        pos["rep"] = lax.axis_index("rep")
        return pos

    def shift(self, name, by):
        if name == "rep":
            return [(i, i + by) for i in range(self.rep) if 0 <= i + by < self.rep]
        step, size = self.stride[name], self.size[name]
        return [
            (i, i + by * step) for i in range(self.dp) if 0 <= (i // step) % size + by < size
        ]

    def flip(self, name):
        return self.shift(name, 1) + self.shift(name, -1)

    def permute(self, value, name, pairs):
        return lax.ppermute(value, "rep" if name == "rep" else "dp", pairs)


def gather_remote(grid, pos, value, name):
    size = grid.size[name]
    if size == 2:
        return grid.permute(value, name, grid.flip(name))[None]
    ups, downs = [], []
    up = down = value
    for _ in range(size - 1):
        up = grid.permute(up, name, grid.shift(name, 1))
        down = grid.permute(down, name, grid.shift(name, -1))
        ups.append(up)
        downs.append(down)
    line = jnp.stack(ups[::-1] + downs)
    return lax.dynamic_slice_in_dim(line, size - 1 - pos[name], size - 1, axis=0)


def insert(own, remote, place):
    count = remote.shape[0] + 1
    rows = []
    for j in range(count):
        if j == 0:
            rows.append(jnp.where(place == 0, own, remote[0]))
        elif j == count - 1:
            rows.append(jnp.where(place == j, own, remote[j - 1]))
        else:
            rows.append(
                jnp.where(place == j, own, jnp.where(place < j, remote[j - 1], remote[j]))
            )
    return jnp.stack(rows)


def gather_axis(grid, pos, value, name):
    if grid.size[name] == 1:
        return value[None]
    return insert(value, gather_remote(grid, pos, value, name), pos[name])


def gather_weight(grid, pos, shard):
    rows, cols = shard.shape
    split = grid.rep == 2 and grid.z > 1 and grid.y == 2
    if not split:
        part = gather_axis(grid, pos, shard, "z")
        part = jnp.moveaxis(gather_axis(grid, pos, part, "y"), 0, 1)
    else:
        half = cols // 2
        mine = lax.dynamic_slice_in_dim(shard, pos["rep"] * half, half, axis=1)
        far = gather_remote(grid, pos, mine, "z")
        near = gather_axis(grid, pos, shard, "y")
        far = jnp.moveaxis(gather_axis(grid, pos, far, "y"), 0, 1)
        other = grid.permute(far, "rep", grid.flip("rep"))
        low = jnp.where(pos["rep"] == 0, far, other)
        high = jnp.where(pos["rep"] == 0, other, far)
        part = insert(near, jnp.concatenate([low, high], axis=-1), pos["z"])
    whole = gather_axis(grid, pos, part, "core")
    return jnp.moveaxis(whole, 0, 2).reshape(grid.dp * rows, cols)


def gather_small(grid, pos, value, names):
    for name in names:
        size = grid.size[name]
        if size & (size - 1) or size == 1:
            if size > 1:
                value = gather_axis(grid, pos, value, name).reshape((-1,) + value.shape[1:])
            continue
        bit = 1
        while bit < size:
            step = bit if name == "rep" else bit * grid.stride[name]
            count = grid.rep if name == "rep" else grid.dp
            other = grid.permute(value, name, [(i, i ^ step) for i in range(count)])
            upper = (pos[name] & bit) > 0
            value = jnp.concatenate(
                [jnp.where(upper, other, value), jnp.where(upper, value, other)], axis=0
            )
            bit *= 2
    return value


def scatter_axis(grid, pos, value, name, kind):
    size = grid.size[name]
    here = pos[name]
    if size == 1:
        return value[0].astype(F32)
    own = lax.dynamic_index_in_dim(value, here, 0, keepdims=False).astype(F32)
    if size == 2:
        out = lax.dynamic_index_in_dim(value, 1 - here, 0, keepdims=False)
        return own + grid.permute(out.astype(kind), name, grid.flip(name)).astype(F32)
    total = own
    for sign in (1, -1):
        arrived = None
        for step in range(1, size):
            target = jnp.clip(here + sign * (size - step), 0, size - 1)
            out = lax.dynamic_index_in_dim(value, target, 0, keepdims=False)
            if arrived is not None:
                out = out.astype(F32) + arrived.astype(F32)
            arrived = grid.permute(out.astype(kind), name, grid.shift(name, sign))
        total = total + arrived.astype(F32)
    return total


def scatter_weight(grid, pos, grad, kind=BF16):
    rows = grad.shape[0] // grid.dp
    cols = grad.shape[1]
    value = grad.astype(kind).reshape(grid.z, grid.y, grid.core, rows, cols)
    value = scatter_axis(grid, pos, jnp.moveaxis(value, 2, 0), "core", kind).astype(kind)
    if grid.rep == 2:
        half = cols // 2
        mine = lax.dynamic_slice_in_dim(value, pos["rep"] * half, half, axis=3)
        theirs = lax.dynamic_slice_in_dim(value, (1 - pos["rep"]) * half, half, axis=3)
        value = mine.astype(F32) + grid.permute(theirs, "rep", grid.flip("rep")).astype(F32)
        value = value.astype(kind)
    value = scatter_axis(grid, pos, jnp.moveaxis(value, 1, 0), "y", kind).astype(kind)
    value = scatter_axis(grid, pos, value, "z", kind)
    if grid.rep == 2:
        value = value.astype(kind)
        other = grid.permute(value, "rep", grid.flip("rep"))
        first = pos["rep"] == 0
        value = jnp.concatenate(
            [jnp.where(first, value, other), jnp.where(first, other, value)], axis=1
        ).astype(F32)
    elif grid.rep > 1:
        value = lax.psum(value, "rep")
    return value


def scatter_small(grid, pos, value):
    shape = value.shape[1:]
    value = value.reshape((grid.z, grid.y, grid.core) + shape)
    value = scatter_axis(grid, pos, jnp.moveaxis(value, 2, 0), "core", F32)
    value = scatter_axis(grid, pos, jnp.moveaxis(value, 1, 0), "y", F32)
    value = scatter_axis(grid, pos, value, "z", F32)
    if grid.rep == 2:
        value = value + grid.permute(value, "rep", grid.flip("rep"))
    elif grid.rep > 1:
        value = lax.psum(value, "rep")
    return value


def mm(left, right):
    return jnp.dot(left, right, preferred_element_type=F32)


def mm_left(left, right):
    return lax.dot_general(left, right, (((0,), (0,)), ((), ())), preferred_element_type=F32)


def mm_back(left, right):
    return lax.dot_general(left, right, (((1,), (1,)), ((), ())), preferred_element_type=F32)


def row_total(values):
    return jnp.sum(values.astype(F32), axis=0)


def norm_parts(v):
    mean_val = jnp.mean(v, axis=-1, keepdims=True)
    centred = v - mean_val
    variance = jnp.mean(centred * centred, axis=-1, keepdims=True)
    scale = lax.rsqrt(variance + 1e-05)
    return centred * scale, scale


def norm_back(grad, unit, scale, gain):
    inner = grad * gain
    mean_one = jnp.mean(inner, axis=-1, keepdims=True)
    mean_two = jnp.mean(inner * unit, axis=-1, keepdims=True)
    return (inner - mean_one - unit * mean_two) * scale


def per_device(
    grid,
    passages,
    lengths,
    queries,
    positives,
    out_grad,
    w_query,
    b_query,
    w_key,
    w_value,
    b_value,
    w_out,
    b_out,
    norm1_gain,
    norm1_bias,
    w_up,
    b_up,
    w_down,
    b_down,
    norm2_gain,
    norm2_bias,
):
    steps, count, length, width = passages.shape
    head = width // H
    total = steps * count
    rows = total * length
    heads = (total, length, H, head)
    score_scale = 1.0 / math.sqrt(head)
    inv_width = 1.0 / math.sqrt(width)
    pos = grid.positions()
    dp = grid.dp

    vectors = (b_query, b_value, b_out, norm1_gain, norm1_bias, b_down, norm2_gain, norm2_bias, b_up)
    small = gather_small(grid, pos, jnp.concatenate(vectors)[None], ("core", "y", "z"))
    spans, at = [], 0
    for vec in vectors:
        spans.append(small[:, at : at + vec.shape[0]].reshape(-1).astype(F32))
        at += vec.shape[0]
    (bias_q, bias_v, bias_out, gain_one, shift_one, bias_down, gain_two, shift_two, bias_up) = spans

    qkv = gather_weight(grid, pos, jnp.concatenate([w_query, w_key, w_value], axis=1))
    weight_q, weight_k, weight_v = qkv[:, :width], qkv[:, width : 2 * width], qkv[:, 2 * width :]
    weight_out = gather_weight(grid, pos, w_out)
    weight_up = gather_weight(grid, pos, w_up)
    weight_down = gather_weight(grid, pos, w_down)
    all_queries = gather_small(
        grid, pos, jnp.moveaxis(queries, 0, 1), ("rep", "core", "y", "z")
    )

    tokens = passages.reshape(rows, width)
    key_valid = (jnp.arange(length)[None, :] < lengths.reshape(total)[:, None])[:, None, None, :]
    q = (mm(tokens, weight_q) + bias_q).astype(BF16).reshape(heads)
    k = mm(tokens, weight_k).astype(BF16).reshape(heads)
    v = (mm(tokens, weight_v) + bias_v).astype(BF16).reshape(heads)

    def scores_of():
        raw = jnp.einsum("plhe,pmhe->phlm", q, k, preferred_element_type=F32) * score_scale
        return jnp.where(key_valid, raw, -1000000000.0)

    scores = scores_of()
    log_total = jax.nn.logsumexp(scores, axis=-1, keepdims=True)
    probs_low = jnp.exp(scores - log_total).astype(BF16)
    context = jnp.einsum("phlm,pmhe->plhe", probs_low, v, preferred_element_type=F32)
    context = context.astype(BF16).reshape(rows, width)
    sum_one = tokens.astype(F32) + mm(context, weight_out) + bias_out
    unit_one, scale_one = norm_parts(sum_one)
    hidden = unit_one * gain_one + shift_one
    hidden_low = hidden.astype(BF16)
    pre = mm(hidden_low, weight_up) + bias_up
    phi = 0.5 * lax.erfc(-pre * INV_SQRT2)
    gelu_low = (pre * phi).astype(BF16)
    slope = (phi + pre * (jnp.exp(-0.5 * pre * pre) * INV_SQRT_2PI)).astype(BF16)
    sum_two = hidden + mm(gelu_low, weight_down) + bias_down
    unit_two, scale_two = norm_parts(sum_two)
    result = (unit_two * gain_two + shift_two).reshape(steps, count, length, width)
    output = result.astype(BF16)

    all_cls = gather_small(
        grid, pos, jnp.moveaxis(output[:, :, 0, :], 0, 1), ("rep", "core", "y", "z")
    )
    first = (pos["z"] * grid.stride["z"] + pos["y"] * grid.stride["y"] + pos["core"]) * grid.rep
    first = (first + pos["rep"]) * count
    logits = jnp.einsum("qmd,pmd->mqp", all_queries, all_cls, preferred_element_type=F32)
    logits = logits * inv_width
    query_total = jax.nn.logsumexp(logits, axis=-1)
    passages_all = all_cls.shape[0]
    mine = lax.dynamic_slice_in_dim(logits, first, count, axis=1)
    mine_total = lax.dynamic_slice_in_dim(query_total, first, count, axis=1)
    onehot = (positives[:, :, None] == jnp.arange(passages_all)[None, None, :]).astype(F32)
    query_loss = mine_total - jnp.sum(mine * onehot, axis=-1)
    mine_grad = (jnp.exp(mine - mine_total[:, :, None]) - onehot) * inv_width
    queries_grad = jnp.einsum(
        "mqp,pmd->mqd", mine_grad.astype(BF16), all_cls, preferred_element_type=F32
    )
    all_positives = gather_small(
        grid, pos, jnp.moveaxis(positives, 0, 1), ("rep", "core", "y", "z")
    )
    column = lax.dynamic_slice_in_dim(logits, first, count, axis=2)
    hit = (all_positives.T[:, :, None] == (first + jnp.arange(count))[None, None, :]).astype(F32)
    column_grad = (jnp.exp(column - query_total[:, :, None]) - hit) * inv_width
    cls_grad = jnp.einsum(
        "mqp,qmd->mpd", column_grad.astype(BF16), all_queries, preferred_element_type=F32
    )

    grad_out = out_grad.astype(F32).at[:, :, 0, :].add(cls_grad).reshape(rows, width)
    grad_gain_two = jnp.sum(grad_out * unit_two, axis=0)
    grad_shift_two = jnp.sum(grad_out, axis=0)
    grad_two = norm_back(grad_out, unit_two, scale_two, gain_two)
    down_low = grad_two.astype(BF16)
    grad_b_down = row_total(down_low)
    shard_w_down = scatter_weight(grid, pos, mm_left(gelu_low, down_low))
    up_low = (mm_back(down_low, weight_down) * slope.astype(F32)).astype(BF16)
    grad_b_up = row_total(up_low)
    shard_w_up = scatter_weight(grid, pos, mm_left(hidden_low, up_low))
    grad_hidden = grad_two + mm_back(up_low, weight_up)
    grad_gain_one = jnp.sum(grad_hidden * unit_one, axis=0)
    grad_shift_one = jnp.sum(grad_hidden, axis=0)
    grad_one = norm_back(grad_hidden, unit_one, scale_one, gain_one)
    attn_low = grad_one.astype(BF16)
    grad_b_out = row_total(attn_low)
    shard_w_out = scatter_weight(grid, pos, mm_left(context, attn_low))
    context_grad = mm_back(attn_low, weight_out).astype(BF16).reshape(heads)
    attn_probs = jnp.exp(scores_of() - log_total)
    probs_grad = jnp.einsum("plhe,pmhe->phlm", context_grad, v, preferred_element_type=F32)
    inner = jnp.sum(probs_grad * attn_probs, axis=-1, keepdims=True)
    score_low = (attn_probs * (probs_grad - inner)).astype(BF16)
    q_low = jnp.einsum("phlm,pmhe->plhe", score_low, k, preferred_element_type=F32) * score_scale
    q_low = q_low.astype(BF16).reshape(rows, width)
    k_low = jnp.einsum("phlm,plhe->pmhe", score_low, q, preferred_element_type=F32) * score_scale
    k_low = k_low.astype(BF16).reshape(rows, width)
    v_low = jnp.einsum("phlm,plhe->pmhe", probs_low, context_grad, preferred_element_type=F32)
    v_low = v_low.astype(BF16).reshape(rows, width)
    shard_w_query = scatter_weight(grid, pos, mm_left(tokens, q_low))
    shard_w_key = scatter_weight(grid, pos, mm_left(tokens, k_low))
    shard_w_value = scatter_weight(grid, pos, mm_left(tokens, v_low))
    grad_b_query = row_total(q_low)
    grad_b_value = row_total(v_low)
    input_grad = (
        grad_one + mm_back(q_low, weight_q) + mm_back(k_low, weight_k) + mm_back(v_low, weight_v)
    )

    grads = (
        grad_b_query,
        grad_b_value,
        grad_b_out,
        grad_gain_one,
        grad_shift_one,
        grad_b_down,
        grad_gain_two,
        grad_shift_two,
        grad_b_up,
    )
    sums = scatter_small(
        grid, pos, jnp.concatenate([g.reshape(dp, -1) for g in grads], axis=1)
    )
    parts, at = [], 0
    for vec in vectors:
        parts.append(sums[at : at + vec.shape[0]])
        at += vec.shape[0]
    (s_b_q, s_b_v, s_b_out, s_gain1, s_shift1, s_b_down, s_gain2, s_shift2, s_b_up) = parts
    return (
        output,
        query_loss,
        input_grad.reshape(steps, count, length, width),
        queries_grad,
        cls_grad,
        shard_w_query,
        s_b_q,
        shard_w_key,
        shard_w_value,
        s_b_v,
        shard_w_out,
        s_b_out,
        s_gain1,
        s_shift1,
        shard_w_up,
        s_b_up,
        shard_w_down,
        s_b_down,
        s_gain2,
        s_shift2,
    )


def solution(mesh):
    both = ("dp", "rep")
    matrix, vector = P("dp", None), P("dp")
    weights = (
        matrix, vector, matrix, matrix, vector, matrix, vector, vector, vector,
        matrix, vector, matrix, vector, vector, vector,
    )
    grid = Grid(mesh.shape["dp"], mesh.shape["rep"])
    wide = P(None, both, None, None)
    return jax.shard_map(
        functools.partial(per_device, grid),
        mesh=mesh,
        in_specs=(wide, P(None, both), P(None, both, None), P(None, both), wide) + weights,
        out_specs=(wide, P(None, both), wide, P(None, both, None), P(None, both, None)) + weights,
        check_vma=False,
    )
```

time: 1220 us -> 661 us (0.54)
  waiting for transfers between devices: 649 us -> 185 us
  blocking collectives: 263 us -> 0 us
  starting transfers between devices: 0.77 us -> 253 us
  local copies, waits for them, and re-layouts: 82.4 us -> 35.3 us
  matrix products: 170 us -> 136 us
  between operations: 19.3 us -> 4.09 us
    reduce_scatter x3 -> x0, waiting for transfers between devices: 294 us -> none  [the longest x1 115 us: per_device(): lax.psum_scatter(total_w_up, 'dp', scatter_dimension=0, tiled=True)]
    ppermute x0 -> x128, starting transfers between devices: none -> 253 us  [permute(): return lax.ppermute(value, 'rep' if name == 'rep' else 'dp', pairs)]
    unnamed x18 -> x0, waiting for transfers between devices: 249 us -> none
    ppermute x0 -> x128, waiting for transfers between devices: none -> 185 us  [permute(): return lax.ppermute(value, 'rep' if name == 'rep' else 'dp', pairs)]
    all_gather x2 -> x0, blocking collectives: 133 us -> none  [per_device(): lax.all_gather(result[:, 0, :].astype(jnp.bfloat16), ('dp', 'rep'), axis=...]
    unnamed x2 -> x0, blocking collectives: 124 us -> none
    all_gather x6 -> x0, waiting for transfers between devices: 106 us -> none  [the longest x1 44.9 us: per_device(): lax.all_gather(w_up, 'dp', axis=0, tiled=True)]
    unnamed x388 -> x161, local copies, waits for them, and re-layouts: 50.9 us -> 5.68 us
  transfers between devices with their start and end apart: 14 -> 128, of which waited for: 10 -> 53; matrix products, arithmetic and copies ran while one was open for 14% -> 18% of each run, Pallas kernels for 0% -> 0%
where the time goes in v1:
time: 661 us; the launch traced here: 654 us
  starting transfers between devices  253 us (38%)
  waiting for transfers between devices  185 us (28%)
  matrix products  136 us (21%)
  other arithmetic  41.2 us (6%)
  local copies, waits for them, and re-layouts  35.3 us (5%)
    ppermute x128, starting transfers between devices, permute(): return lax.ppermute(value, 'rep' if name == 'rep' else 'dp', pairs)  253 us
    ppermute x128, waiting for transfers between devices, permute(): return lax.ppermute(value, 'rep' if name == 'rep' else 'dp', pairs)  185 us
    dot_general x6, matrix products, mm(): return jnp.dot(left, right, preferred_element_type=F32)  46.9 us
    dot_general x6, matrix products, mm_back(): lax.dot_general(left, right, (((1,), (1,)), ((), ())), preferred_element_...  40.1 us
    dot_general x6, matrix products, mm_left(): lax.dot_general(left, right, (((0,), (0,)), ((), ())), preferred_element_...  31.2 us
  transfers between devices with their start and end apart: 128, of which 53 were waited for; matrix products, arithmetic and copies ran while one was open for 18% of the time, Pallas kernels for 0%

profile of v1, /device:TPU:0, one launch (start us, length us, event | category | flops | bytes accessed | tf_op | source)
XLA Modules:
  0.0 654.0 jit_solution(16366819914726544171)
XLA Ops:
  1.7 4.9 collective-permute-start.35
  17.6 6.1 concatenate.135
  69.8 4.9 collective-permute-start.17
  77.7 4.8 collective-permute-done.20
  84.6 6.7 %collective-permute-done.21 = bf16[3,48,384]{2,1,0:T(8,128)(2,1)S(1)} collective-permute-done((bf16[3,48,384]{2,1,0:T(8,128)(2,1)S(1)}, bf16[3,48,384]{2,1,0:T(8,128)(2,1)S(1)}, u32[]{:S(2)}, u32[]{:S(2)}) %collective-permute-start.21) | collective-permute-done | bytes 110624 | tf_op jit(solution)/shard_map/ppermute | solution.py:46
  98.6 5.0 collective-permute-start.2
  124.0 5.2 collective-permute-start.26
  153.6 6.6 %collective-permute-done.41 = bf16[3,192,384]{2,1,0:T(8,128)(2,1)S(1)} collective-permute-done((bf16[3,192,384]{2,1,0:T(8,128)(2,1)S(1)}, bf16[3,192,384]{2,1,0:T(8,128)(2,1)S(1)}, u32[]{:S(2)}, u32[]{:S(2)}) %collective-permute-start.41) | collective-permute-done | bytes 442400 | tf_op jit(solution)/shard_map/ppermute | solution.py:46
  170.9 18.1 %collective-permute-done.42 = bf16[3,2,192,384]{3,2,1,0:T(8,128)(2,1)S(1)} collective-permute-done((bf16[3,2,192,384]{3,2,1,0:T(8,128)(2,1)S(1)}, bf16[3,2,192,384]{3,2,1,0:T(8,128)(2,1)S(1)}, u32[]{:S(2)}, u32[]{:S(2)}) %collective-permute-start.42) | collective-permute-done | bytes 884768 | tf_op jit(solution)/shard_map/ppermute | solution.py:46
  190.2 12.4 %collective-permute-done.32 = bf16[3,2,48,1536]{3,2,1,0:T(8,128)(2,1)S(1)} collective-permute-done((bf16[3,2,48,1536]{3,2,1,0:T(8,128)(2,1)S(1)}, bf16[3,2,48,1536]{3,2,1,0:T(8,128)(2,1)S(1)}, u32[]{:S(2)}, u32[]{:S(2)}) %collective-permute-start.32) | collective-permute-done | bytes 884768 | tf_op jit(solution)/shard_map/ppermute | solution.py:46
  222.9 35.2 %multiply_convert_fusion.1 = (bf16[1024,3072]{1,0:T(8,128)(2,1)S(1)}, f32[1024,3072]{1,0:T(8,128)}, f32[1024,3072]{1,0:T(8,128)}) fusion(f32[3072]{0:T(1024)S(1)} %reshape.584, bf16[768,3072]{1,0:T(8,128)(2,1)S(1)} %bitcast.512, f32[1024,768]{1,0:T(8,128)S(1)} %get-tuple-element.208, f32[768]{0:T(1024)S(1)} %reshape.583, f32[768]{0:T(1024)S(1)} %reshape.582, ...), kind=kOutput, calls=%fused_computation.11 | convolution fusion | flops 5043388416 | bytes 39348224 | tf_op jit(solution)/shard_map/dot_general | solution.py:186
  258.2 5.4 fusion.193
  284.9 9.3 %collective-permute-done.48 = bf16[64,2,768]{2,0,1:T(8,128)(2,1)S(1)} collective-permute-done((bf16[64,2,768]{2,0,1:T(8,128)(2,1)S(1)}, bf16[64,2,768]{2,0,1:T(8,128)(2,1)S(1)}, u32[]{:S(2)}, u32[]{:S(2)}) %collective-permute-start.48) | collective-permute-done | bytes 196640 | tf_op jit(solution)/shard_map/ppermute | solution.py:46
  304.7 11.0 %convolution_convert_fusion = bf16[3072,768]{1,0:T(8,128)(2,1)} fusion(bf16[1024,3072]{1,0:T(8,128)(2,1)} %copy-done.59, f32[1024,768]{1,0:T(8,128)S(1)} %get-tuple-element.48), kind=kOutput, calls=%fused_computation.31 | convolution fusion | flops 4834983936 | bytes 14155776 | tf_op jit(solution)/shard_map/dot_general | solution.py:190
  315.8 17.0 %convert_reduce_fusion = (f32[3072]{0:T(1024)S(1)}, bf16[1024,3072]{1,0:T(8,128)(2,1)}) fusion(f32[1024,3072]{1,0:T(8,128)} %get-tuple-element.54, f32[1024,3072]{1,0:T(8,128)} %get-tuple-element.209, f32[3072]{0:T(1024)S(1)} %reshape.584, bf16[3072,768]{1,0:T(8,128)(2,1)} %bitcast.511, f32[1024,768]{1,0:T(8,128)} %copy-done.20), kind=kOutput, calls=%fused_computation.9 | convolution fusion | flops 4870370304 | bytes 39346176 | tf_op jit(solution)/shard_map/dot_general | solution.py:194
  332.8 10.2 %convolution_convert_fusion.1 = bf16[768,3072]{1,0:T(8,128)(2,1)} fusion(bf16[1024,3072]{1,0:T(8,128)(2,1)} %get-tuple-element.224, f32[1024,768]{1,0:T(8,128)S(1)} %copy-done.4, f32[768]{0:T(1024)S(1)} %reshape.583, f32[768]{0:T(1024)S(1)} %reshape.582, f32[1024]{0:T(1024)S(1)} %add_rsqrt_fusion.1, f32[1024]{0:T(1024)S(1)} %broadcast_multiply_fusion.5), kind=kOutput, calls=%fused_computation.32 | convolution fusion | flops 4838129664 | bytes 14170112 | tf_op jit(solution)/shard_map/dot_general | solution.py:190
  343.0 8.4 %multiply_reduce_fusion.1 = (f32[768]{0:T(1024)S(1)}, f32[1024]{0:T(1024)S(1)}, f32[1024]{0:T(1024)S(1)}, f32[768]{0:T(1024)S(1)}, f32[1024,768]{1,0:T(8,128)S(1)}) fusion(f32[1024,768]{1,0:T(8,128)S(1)} %copy-done.4, f32[1024]{0:T(1024)S(1)} %add_rsqrt_fusion.1, f32[1024]{0:T(1024)S(1)} %broadcast_multiply_fusion.5, f32[768]{0:T(1024)S(1)} %reshape.582, ...), kind=kOutput, calls=%fused_computation.46 | convolution fusion | flops 4839698432 | bytes 20472832 | tf_op jit(solution)/shard_map/dot_general | solution.py:194
  358.0 5.4 convert_reduce_fusion.3
  401.5 7.0 %add_add_fusion = f32[1024,768]{1,0:T(8,128)} fusion(f32[1024,768]{1,0:T(8,128)} %fusion.24, f32[1024,768]{1,0:T(8,128)S(1)} %copy-done.6, f32[1024,768]{1,0:T(8,128)} %fusion.28, bf16[96,8,8,128]{3,2,1,0:T(8,128)(2,1)} %bitcast.494, bf16[768,2304]{1,0:T(8,128)(2,1)} %bitcast.503), kind=kOutput, calls=%fused_computation.50 | convolution fusion | flops 1210318848 | bytes 15335424 | tf_op jit(solution)/shard_map/dot_general | solution.py:194
  443.6 5.6 collective-permute-done.99
  450.8 4.7 collective-permute-done.89
  456.6 5.3 collective-permute-done.79
  569.6 21.1 %collective-permute-done.119 = bf16[4,2,192,384]{3,2,0,1:T(8,128)(2,1)S(1)} collective-permute-done((bf16[4,2,192,384]{3,2,0,1:T(8,128)(2,1)S(1)}, bf16[4,2,192,384]{3,2,0,1:T(8,128)(2,1)S(1)}, u32[]{:S(2)}, u32[]{:S(2)}) %collective-permute-start.119) | collective-permute-done | bytes 1179680 | tf_op jit(solution)/shard_map/ppermute | solution.py:46
  592.1 11.3 %collective-permute-done.109 = bf16[4,2,48,1536]{3,2,0,1:T(8,128)(2,1)S(1)} collective-permute-done((bf16[4,2,48,1536]{3,2,0,1:T(8,128)(2,1)S(1)}, bf16[4,2,48,1536]{3,2,0,1:T(8,128)(2,1)S(1)}, u32[]{:S(2)}, u32[]{:S(2)}) %collective-permute-start.109) | collective-permute-done | bytes 1179680 | tf_op jit(solution)/shard_map/ppermute | solution.py:46
  (662 shorter events, 418.3 us)
Async XLA Ops:
  1.7 112.5 %collective-permute-start.35 = (bf16[192,384]{1,0:T(8,128)(2,1)S(1)}, bf16[192,384]{1,0:T(8,128)(2,1)S(1)}, u32[]{:S(2)}, u32[]{:S(2)}) collective-permute-start(bf16[192,384]{1,0:T(8,128)(2,1)S(1)} %constant_dynamic-slice_fusion.32), channel_id=1, source_target_pairs={{0,8},{2,10},{4,12},{6,14},{8,16},{10,18},{12,20},{14,22},{16,24},... | collective-permute-start | bytes 442376 | tf_op jit(solution)/shard_map/ppermute | solution.py:46
  6.7 114.9 %collective-permute-start.38 = (bf16[192,384]{1,0:T(8,128)(2,1)S(1)}, bf16[192,384]{1,0:T(8,128)(2,1)S(1)}, u32[]{:S(2)}, u32[]{:S(2)}) collective-permute-start(bf16[192,384]{1,0:T(8,128)(2,1)S(1)} %constant_dynamic-slice_fusion.32), channel_id=1, source_target_pairs={{8,0},{10,2},{12,4},{14,6},{16,8},{18,10},{20,12},{22,14},{24,16},... | collective-permute-start | bytes 442376 | tf_op jit(solution)/shard_map/ppermute | solution.py:46
  8.7 52.8 %collective-permute-start.15 = (bf16[48,384]{1,0:T(8,128)(2,1)S(1)}, bf16[48,384]{1,0:T(8,128)(2,1)S(1)}, u32[]{:S(2)}, u32[]{:S(2)}) collective-permute-start(bf16[48,384]{1,0:T(8,128)(2,1)S(1)} %constant_dynamic-slice_fusion.36), channel_id=1, source_target_pairs={{0,8},{2,10},{4,12},{6,14},{8,16},{10,18},{12,20},{14,22},{16,24},... | collective-permute-start | bytes 110600 | tf_op jit(solution)/shard_map/ppermute | solution.py:46
  13.3 54.3 %collective-permute-start.18 = (bf16[48,384]{1,0:T(8,128)(2,1)S(1)}, bf16[48,384]{1,0:T(8,128)(2,1)S(1)}, u32[]{:S(2)}, u32[]{:S(2)}) collective-permute-start(bf16[48,384]{1,0:T(8,128)(2,1)S(1)} %constant_dynamic-slice_fusion.36), channel_id=1, source_target_pairs={{8,0},{10,2},{12,4},{14,6},{16,8},{18,10},{20,12},{22,14},{24,16},... | collective-permute-start | bytes 110600 | tf_op jit(solution)/shard_map/ppermute | solution.py:46
  67.6 42.0 %collective-permute-start.34 = (bf16[192,768]{1,0:T(8,128)(2,1)S(1)}, bf16[192,768]{1,0:T(8,128)(2,1)S(1)}, u32[]{:S(2)}, u32[]{:S(2)}) collective-permute-start(bf16[192,768]{1,0:T(8,128)(2,1)S(1)} %copy-done.33), channel_id=1, source_target_pairs={{0,4},{2,6},{8,12},{10,14},{16,20},{18,22},{24,28},{26,30},{4,0},{... | collective-permute-start | bytes 884744 | tf_op jit(solution)/shard_map/ppermute | solution.py:46
  104.4 18.3 %collective-permute-start.25 = (bf16[48,1536]{1,0:T(8,128)(2,1)S(1)}, bf16[48,1536]{1,0:T(8,128)(2,1)S(1)}, u32[]{:S(2)}, u32[]{:S(2)}) collective-permute-start(bf16[48,1536]{1,0:T(8,128)(2,1)S(1)} %constant_dynamic-slice_fusion.34), channel_id=1, source_target_pairs={{0,8},{2,10},{4,12},{6,14},{8,16},{10,18},{12,20},{14,22},{16,24},... | collective-permute-start | bytes 442376 | tf_op jit(solution)/shard_map/ppermute | solution.py:46
  121.5 145.0 %collective-permute-start.46 = (bf16[16,2,768]{2,0,1:T(8,128)(2,1)}, bf16[16,2,768]{2,0,1:T(8,128)(2,1)}, u32[]{:S(2)}, u32[]{:S(2)}) collective-permute-start(bf16[16,2,768]{2,0,1:T(8,128)(2,1)} %pad_maximum_fusion.26), channel_id=1, source_target_pairs={{0,4},{2,6},{4,0},{6,2},{8,12},{10,14},{12,8},{14,10},{16,20},{18,... | collective-permute-start | bytes 147464 | tf_op jit(solution)/shard_map/ppermute | solution.py:46
  146.2 20.5 %collective-permute-start.23 = (bf16[4,2,48,768]{3,2,1,0:T(8,128)(2,1)S(1)}, bf16[4,2,48,768]{3,2,1,0:T(8,128)(2,1)S(1)}, u32[]{:S(2)}, u32[]{:S(2)}) collective-permute-start(bf16[4,2,48,768]{3,2,1,0:T(8,128)(2,1)S(1)} %pad_maximum_fusion.9), channel_id=1, source_target_pairs={{0,2},{4,6},{8,10},{12,14},{16,18},{20,22},{24,26},{28,30},{2,0},{... | collective-permute-start | bytes 1769480 | tf_op jit(solution)/shard_map/ppermute | solution.py:46
  160.5 28.5 %collective-permute-start.42 = (bf16[3,2,192,384]{3,2,1,0:T(8,128)(2,1)S(1)}, bf16[3,2,192,384]{3,2,1,0:T(8,128)(2,1)S(1)}, u32[]{:S(2)}, u32[]{:S(2)}) collective-permute-start(bf16[3,2,192,384]{3,2,1,0:T(8,128)(2,1)S(1)} %maximum_bitcast_fusion.1), channel_id=1, source_target_pairs={{0,1},{1,0},{2,3},{3,2},{4,5},{5,4},{6,7},{7,6},{8,9},{9,8},{10,11... | collective-permute-start | bytes 2654216 | tf_op jit(solution)/shard_map/ppermute | solution.py:46
  165.2 37.4 %collective-permute-start.32 = (bf16[3,2,48,1536]{3,2,1,0:T(8,128)(2,1)S(1)}, bf16[3,2,48,1536]{3,2,1,0:T(8,128)(2,1)S(1)}, u32[]{:S(2)}, u32[]{:S(2)}) collective-permute-start(bf16[3,2,48,1536]{3,2,1,0:T(8,128)(2,1)S(1)} %maximum_bitcast_fusion), channel_id=1, source_target_pairs={{0,1},{1,0},{2,3},{3,2},{4,5},{5,4},{6,7},{7,6},{8,9},{9,8},{10,11... | collective-permute-start | bytes 2654216 | tf_op jit(solution)/shard_map/ppermute | solution.py:46
  170.8 32.9 %collective-permute-start.9 = (bf16[4,2,48,2304]{3,2,1,0:T(8,128)(2,1)S(1)}, bf16[4,2,48,2304]{3,2,1,0:T(8,128)(2,1)S(1)}, u32[]{:S(2)}, u32[]{:S(2)}) collective-permute-start(bf16[4,2,48,2304]{3,2,1,0:T(8,128)(2,1)S(1)} %pad_maximum_fusion.5), channel_id=1, source_target_pairs={{0,2},{4,6},{8,10},{12,14},{16,18},{20,22},{24,26},{28,30},{2,0},{... | collective-permute-start | bytes 5308424 | tf_op jit(solution)/shard_map/ppermute | solution.py:46
  190.1 30.9 %collective-permute-start.43 = (bf16[4,2,192,768]{3,2,1,0:T(8,128)(2,1)S(1)}, bf16[4,2,192,768]{3,2,1,0:T(8,128)(2,1)S(1)}, u32[]{:S(2)}, u32[]{:S(2)}) collective-permute-start(bf16[4,2,192,768]{3,2,1,0:T(8,128)(2,1)S(1)} %pad_maximum_fusion.4), channel_id=1, source_target_pairs={{0,2},{4,6},{8,10},{12,14},{16,18},{20,22},{24,26},{28,30},{2,0},{... | collective-permute-start | bytes 7077896 | tf_op jit(solution)/shard_map/ppermute | solution.py:46
  203.6 18.3 %collective-permute-start.33 = (bf16[4,2,48,3072]{3,2,1,0:T(8,128)(2,1)S(1)}, bf16[4,2,48,3072]{3,2,1,0:T(8,128)(2,1)S(1)}, u32[]{:S(2)}, u32[]{:S(2)}) collective-permute-start(bf16[4,2,48,3072]{3,2,1,0:T(8,128)(2,1)S(1)} %pad_maximum_fusion.3), channel_id=1, source_target_pairs={{0,2},{4,6},{8,10},{12,14},{16,18},{20,22},{24,26},{28,30},{2,0},{... | collective-permute-start | bytes 7077896 | tf_op jit(solution)/shard_map/ppermute | solution.py:46
  390.0 170.8 %collective-permute-start.118 = (bf16[4,2,192,768]{3,2,0,1:T(8,128)(2,1)}, bf16[4,2,192,768]{3,2,0,1:T(8,128)(2,1)}, u32[]{:S(2)}, u32[]{:S(2)}) collective-permute-start(bf16[4,2,192,768]{3,2,0,1:T(8,128)(2,1)} %bitcast.482), channel_id=1, source_target_pairs={{0,2},{4,6},{8,10},{12,14},{16,18},{20,22},{24,26},{28,30},{2,0},{... | collective-permute-start | bytes 7077896 | tf_op jit(solution)/shard_map/ppermute | solution.py:46
  393.8 170.1 %collective-permute-start.108 = (bf16[4,2,48,3072]{3,2,0,1:T(8,128)(2,1)}, bf16[4,2,48,3072]{3,2,0,1:T(8,128)(2,1)}, u32[]{:S(2)}, u32[]{:S(2)}) collective-permute-start(bf16[4,2,48,3072]{3,2,0,1:T(8,128)(2,1)} %bitcast.483), channel_id=1, source_target_pairs={{0,2},{4,6},{8,10},{12,14},{16,18},{20,22},{24,26},{28,30},{2,0},{... | collective-permute-start | bytes 7077896 | tf_op jit(solution)/shard_map/ppermute | solution.py:46
  396.1 41.4 %collective-permute-start.98 = (bf16[4,2,48,768]{3,2,0,1:T(8,128)(2,1)}, bf16[4,2,48,768]{3,2,0,1:T(8,128)(2,1)}, u32[]{:S(2)}, u32[]{:S(2)}) collective-permute-start(bf16[4,2,48,768]{3,2,0,1:T(8,128)(2,1)} %bitcast.484), channel_id=1, source_target_pairs={{0,2},{4,6},{8,10},{12,14},{16,18},{20,22},{24,26},{28,30},{2,0},{... | collective-permute-start | bytes 1769480 | tf_op jit(solution)/shard_map/ppermute | solution.py:46
  441.8 20.0 %collective-permute-start.79 = (bf16[4,2,48,384]{3,2,0,1:T(8,128)(2,1)S(1)}, bf16[4,2,48,384]{3,2,0,1:T(8,128)(2,1)S(1)}, u32[]{:S(2)}, u32[]{:S(2)}) collective-permute-start(bf16[4,2,48,384]{3,2,0,1:T(8,128)(2,1)S(1)} %constant_dynamic-slice_fusion.12), channel_id=1, source_target_pairs={{0,1},{1,0},{2,3},{3,2},{4,5},{5,4},{6,7},{7,6},{8,9},{9,8},{10,11... | collective-permute-start | bytes 884744 | tf_op jit(solution)/shard_map/ppermute | solution.py:46
  449.2 18.0 %collective-permute-start.60 = (bf16[4,2,48,384]{3,2,0,1:T(8,128)(2,1)S(1)}, bf16[4,2,48,384]{3,2,0,1:T(8,128)(2,1)S(1)}, u32[]{:S(2)}, u32[]{:S(2)}) collective-permute-start(bf16[4,2,48,384]{3,2,0,1:T(8,128)(2,1)S(1)} %constant_dynamic-slice_fusion.26), channel_id=1, source_target_pairs={{0,1},{1,0},{2,3},{3,2},{4,5},{5,4},{6,7},{7,6},{8,9},{9,8},{10,11... | collective-permute-start | bytes 884744 | tf_op jit(solution)/shard_map/ppermute | solution.py:46
  473.8 24.0 %collective-permute-start.104 = (bf16[48,384]{1,0:T(8,128)(2,1)S(1)}, bf16[48,384]{1,0:T(8,128)(2,1)S(1)}, u32[]{:S(2)}, u32[]{:S(2)}) collective-permute-start(bf16[48,384]{1,0:T(8,128)(2,1)S(1)} %get-tuple-element.132), channel_id=1, source_target_pairs={{8,0},{10,2},{12,4},{14,6},{16,8},{18,10},{20,12},{22,14},{24,16},... | collective-permute-start | bytes 110600 | tf_op jit(solution)/shard_map/ppermute | solution.py:46
  479.8 23.8 %collective-permute-start.94 = (bf16[48,384]{1,0:T(8,128)(2,1)S(1)}, bf16[48,384]{1,0:T(8,128)(2,1)S(1)}, u32[]{:S(2)}, u32[]{:S(2)}) collective-permute-start(bf16[48,384]{1,0:T(8,128)(2,1)S(1)} %get-tuple-element.136), channel_id=1, source_target_pairs={{8,0},{10,2},{12,4},{14,6},{16,8},{18,10},{20,12},{22,14},{24,16},... | collective-permute-start | bytes 110600 | tf_op jit(solution)/shard_map/ppermute | solution.py:46
  514.8 23.8 %collective-permute-start.103 = (bf16[48,384]{1,0:T(8,128)(2,1)S(1)}, bf16[48,384]{1,0:T(8,128)(2,1)S(1)}, u32[]{:S(2)}, u32[]{:S(2)}) collective-permute-start(bf16[48,384]{1,0:T(8,128)(2,1)S(1)} %get-tuple-element.129), channel_id=1, source_target_pairs={{0,8},{2,10},{4,12},{6,14},{8,16},{10,18},{12,20},{14,22},{16,24},... | collective-permute-start | bytes 110600 | tf_op jit(solution)/shard_map/ppermute | solution.py:46
  520.7 23.8 %collective-permute-start.93 = (bf16[48,384]{1,0:T(8,128)(2,1)S(1)}, bf16[48,384]{1,0:T(8,128)(2,1)S(1)}, u32[]{:S(2)}, u32[]{:S(2)}) collective-permute-start(bf16[48,384]{1,0:T(8,128)(2,1)S(1)} %get-tuple-element.133), channel_id=1, source_target_pairs={{0,8},{2,10},{4,12},{6,14},{8,16},{10,18},{12,20},{14,22},{16,24},... | collective-permute-start | bytes 110600 | tf_op jit(solution)/shard_map/ppermute | solution.py:46
  563.3 27.4 %collective-permute-start.119 = (bf16[4,2,192,384]{3,2,0,1:T(8,128)(2,1)S(1)}, bf16[4,2,192,384]{3,2,0,1:T(8,128)(2,1)S(1)}, u32[]{:S(2)}, u32[]{:S(2)}) collective-permute-start(bf16[4,2,192,384]{3,2,0,1:T(8,128)(2,1)S(1)} %constant_dynamic-slice_fusion), channel_id=1, source_target_pairs={{0,1},{1,0},{2,3},{3,2},{4,5},{5,4},{6,7},{7,6},{8,9},{9,8},{10,11... | collective-permute-start | bytes 3538952 | tf_op jit(solution)/shard_map/ppermute | solution.py:46
  566.7 36.7 %collective-permute-start.109 = (bf16[4,2,48,1536]{3,2,0,1:T(8,128)(2,1)S(1)}, bf16[4,2,48,1536]{3,2,0,1:T(8,128)(2,1)S(1)}, u32[]{:S(2)}, u32[]{:S(2)}) collective-permute-start(bf16[4,2,48,1536]{3,2,0,1:T(8,128)(2,1)S(1)} %constant_dynamic-slice_fusion.3), channel_id=1, source_target_pairs={{0,1},{1,0},{2,3},{3,2},{4,5},{5,4},{6,7},{7,6},{8,9},{9,8},{10,11... | collective-permute-start | bytes 3538952 | tf_op jit(solution)/shard_map/ppermute | solution.py:46
  (170 other events, 1978.3 us)

commit v2 on v1

v2 whole, which is shorter than its diff:
```python
import functools
import math

import jax
import jax.numpy as jnp
from jax import lax
from jax.experimental import pallas as pl
from jax.experimental.pallas import tpu as pltpu
from jax.sharding import PartitionSpec as P

H = 12
F32 = jnp.float32
BF16 = jnp.bfloat16
INV_SQRT2 = 1.0 / math.sqrt(2.0)
INV_SQRT_2PI = 1.0 / math.sqrt(2.0 * math.pi)


ANY = pl.BlockSpec(memory_space=pl.ANY)
SMEM = pl.BlockSpec(memory_space=pltpu.SMEM)
VMEM = pl.BlockSpec(memory_space=pltpu.VMEM)
MIB = 2**20
LANES = 128


class Grid:
    def __init__(self, dp, rep, rows):
        self.dp, self.rep = dp, rep
        self.fast = dp == 16 and rep == 2 and rows % 16 == 0
        self.bits = {"core": 1, "y": 2, "z1": 4, "z2": 8}

    def flip(self, value, name):
        if name == "x":
            return lax.ppermute(value, "rep", [(i, i ^ 1) for i in range(self.rep)])
        bit = self.bits[name]
        return lax.ppermute(value, "dp", [(i, i ^ bit) for i in range(self.dp)])


def run_copies(copies):
    for copy in copies:
        copy.start()
    for copy in copies:
        copy.wait()


def place_of(here_ref, key, rows):
    core, y, z, half = key
    row = pl.multiple_of((here_ref[0] ^ (z * 4 + y * 2 + core)) * rows, 16)
    return pl.ds(row, rows), here_ref[1] ^ half


def join_kernel(here_ref, *refs, keys, widths, extra):
    count = len(keys)
    pieces, outs, sems = refs[:count], refs[count:-1], refs[-1]
    copies = []
    for piece, names in zip(pieces, keys):
        for i, key in enumerate(names):
            rows = piece.shape[1]
            where, half = place_of(here_ref, key, rows)
            at = 0
            for out, width in zip(outs, widths):
                column = pl.ds(pl.multiple_of(half * width, LANES), width)
                copies.append((piece.at[i, :, pl.ds(at, width)], out.at[where, column]))
                at += width
            if extra and key[3] == 0:
                copies.append((piece.at[i, :, pl.ds(at, extra)], outs[-1].at[where, :]))
    run_copies([pltpu.make_async_copy(a, b, sems.at[i]) for i, (a, b) in enumerate(copies)])


def join(bag, widths, extra, here):
    arrays, keys = zip(*bag)
    rows = arrays[0].shape[1]
    shapes = [(16 * rows, 2 * width) for width in widths] + ([(16 * rows, extra)] if extra else [])
    copies = 32 * len(widths) + (16 if extra else 0)
    size = sum(a * b for a, b in shapes)
    return pl.pallas_call(
        functools.partial(join_kernel, keys=keys, widths=widths, extra=extra),
        out_shape=[jax.ShapeDtypeStruct(shape, arrays[0].dtype) for shape in shapes],
        in_specs=[SMEM] + [ANY] * len(arrays),
        out_specs=[VMEM] * len(shapes),
        scratch_shapes=[pltpu.SemaphoreType.DMA((copies,))],
        compiler_params=pltpu.CompilerParams(vmem_limit_bytes=32 * MIB),
        cost_estimate=pl.CostEstimate(flops=0, bytes_accessed=4 * size, transcendentals=0),
        name="join",
    )(here, *arrays)


def split_kernel(here_ref, value_ref, *refs, keys):
    *pieces, sems = refs
    copies = []
    for piece, names in zip(pieces, keys):
        _, rows, width = piece.shape
        for i, key in enumerate(names):
            where, half = place_of(here_ref, key, rows)
            column = pl.ds(pl.multiple_of(half * width, LANES), width)
            copies.append((value_ref.at[where, column], piece.at[i]))
    run_copies([pltpu.make_async_copy(a, b, sems.at[i]) for i, (a, b) in enumerate(copies)])


def split(value, keys, here):
    rows, width = value.shape[0] // 16, value.shape[1] // 2
    return pl.pallas_call(
        functools.partial(split_kernel, keys=keys),
        out_shape=[jax.ShapeDtypeStruct((len(names), rows, width), value.dtype) for names in keys],
        in_specs=[SMEM, VMEM],
        out_specs=[ANY] * len(keys),
        scratch_shapes=[pltpu.SemaphoreType.DMA((32,))],
        compiler_params=pltpu.CompilerParams(vmem_limit_bytes=32 * MIB),
        cost_estimate=pl.CostEstimate(flops=0, bytes_accessed=4 * value.size, transcendentals=0),
        name="split",
    )(here, value)


def halves_of(parts, extra, x):
    out = []
    for place in (x, 1 - x):
        row = [
            lax.dynamic_slice_in_dim(p, place * (p.shape[1] // 2), p.shape[1] // 2, axis=1)
            for p in parts
        ]
        out.append(jnp.concatenate(row + ([extra] if extra is not None else []), axis=1))
    return out


def with_cores(grid, bag):
    return bag + [(grid.flip(a, "core"), [(1,) + k[1:] for k in keys]) for a, keys in bag]


def gather_first(grid, here, parts, extra):
    mine, twin = halves_of(parts, extra, here[1])
    own = jnp.stack([mine, twin])
    h0 = mine[None]
    across = grid.flip(own, "y")
    h1 = grid.flip(h0, "z1")
    h2 = grid.flip(h0, "z2")
    line = jnp.concatenate([h1, h2])
    h3 = grid.flip(h1, "z2")
    line_y = grid.flip(line, "y")
    line_x = grid.flip(line, "x")
    back_y = grid.flip(jnp.concatenate([h3, line_x[:1]]), "y")
    back_x = grid.flip(jnp.concatenate([h3, line_y[1:]]), "x")
    last = grid.flip(back_y[:1], "x")
    bag = [
        (own, [(0, 0, 0, 0), (0, 0, 0, 1)]),
        (across, [(0, 1, 0, 0), (0, 1, 0, 1)]),
        (line, [(0, 0, 1, 0), (0, 0, 2, 0)]),
        (line_y, [(0, 1, 1, 0), (0, 1, 2, 0)]),
        (line_x, [(0, 0, 1, 1), (0, 0, 2, 1)]),
        (h3, [(0, 0, 3, 0)]),
        (back_y, [(0, 1, 3, 0), (0, 1, 1, 1)]),
        (back_x, [(0, 0, 3, 1), (0, 1, 2, 1)]),
        (last, [(0, 1, 3, 1)]),
    ]
    widths = [p.shape[1] // 2 for p in parts]
    return join(with_cores(grid, bag), widths, extra.shape[1], here)


def gather_later(grid, here, parts):
    mine = halves_of(parts, None, here[1])[0][None]
    low = jnp.concatenate([mine, grid.flip(mine, "z1")])
    line = jnp.concatenate([low, grid.flip(low, "z2")])
    line_y = grid.flip(line, "y")
    line_x = grid.flip(line, "x")
    cross_x = grid.flip(line_y[:2], "x")
    cross_y = grid.flip(line_x[2:], "y")
    bag = [
        (line, [(0, 0, z, 0) for z in range(4)]),
        (line_y, [(0, 1, z, 0) for z in range(4)]),
        (line_x, [(0, 0, z, 1) for z in range(4)]),
        (cross_x, [(0, 1, z, 1) for z in range(2)]),
        (cross_y, [(0, 1, z, 1) for z in range(2, 4)]),
    ]
    return join(with_cores(grid, bag), [p.shape[1] // 2 for p in parts], 0, here)


def gather_small(grid, value):
    if not grid.fast:
        return lax.all_gather(value, ("dp", "rep"), axis=0, tiled=True)
    for name in ("x", "core", "y", "z1", "z2"):
        other = grid.flip(value, name)
        if name == "x":
            upper = lax.axis_index("rep") > 0
        else:
            upper = (lax.axis_index("dp") & grid.bits[name]) > 0
        value = jnp.concatenate(
            [jnp.where(upper, other, value), jnp.where(upper, value, other)], axis=0
        )
    return value


def added(kind, *terms):
    total = terms[0].astype(F32)
    for term in terms[1:]:
        total = total + term.astype(F32)
    return total.astype(kind)


def scatter_weight(grid, here, grad):
    if not grid.fast:
        part = lax.psum_scatter(grad.astype(F32), "dp", scatter_dimension=0, tiled=True)
        return lax.psum(part, "rep")
    low, high = (0, 1), (2, 3)
    names = [(1, 1, low), (1, 1, high), (0, 1, low), (0, 1, high), (1, 0, low), (1, 0, high)]
    names = names + [(0, 0, low + high)]
    keys = [[(c, y, z, h) for z in zs] for c in range(2) for y, h, zs in names]
    pieces = split(grad.astype(BF16), keys, here)
    count = len(names)
    far = [grid.flip(p, "core") for p in pieces[count:]]
    (cross_low, cross_high, x_low, x_high, y_low, y_high, own) = list(zip(pieces, far))
    got_y_low = grid.flip(added(BF16, *cross_low), "x")
    got_x_high = grid.flip(added(BF16, *cross_high), "y")
    to_x = jnp.concatenate([added(BF16, *x_low), added(BF16, *x_high, got_x_high)])
    to_y = jnp.concatenate([added(BF16, *y_low, got_y_low), added(BF16, *y_high)])
    value = added(BF16, *own, grid.flip(to_x, "x"), grid.flip(to_y, "y"))
    value = added(BF16, value[:2], grid.flip(value[2:], "z2"))
    value = added(BF16, value[0], grid.flip(value[1], "z1"))
    other = grid.flip(value, "x")
    first = here[1] == 0
    return jnp.concatenate(
        [jnp.where(first, value, other), jnp.where(first, other, value)], axis=1
    ).astype(F32)


def scatter_small(grid, value, mine):
    if not grid.fast:
        return mine(lax.psum(value, ("dp", "rep")))
    for name in ("x", "core", "y", "z1", "z2"):
        value = value + grid.flip(value, name)
    return mine(value)


def mm(left, right):
    return jnp.dot(left, right, preferred_element_type=F32)


def mm_left(left, right):
    return lax.dot_general(left, right, (((0,), (0,)), ((), ())), preferred_element_type=F32)


def mm_back(left, right):
    return lax.dot_general(left, right, (((1,), (1,)), ((), ())), preferred_element_type=F32)


def row_total(values):
    return jnp.sum(values.astype(F32), axis=0)


def normal_parts(v):
    phi = 0.5 + 0.5 * lax.erf(v * INV_SQRT2)
    return phi, jnp.exp(-0.5 * v * v) * INV_SQRT_2PI


def norm_parts(v):
    mean_val = jnp.mean(v, axis=-1, keepdims=True)
    centred = v - mean_val
    variance = jnp.mean(centred * centred, axis=-1, keepdims=True)
    scale = lax.rsqrt(variance + 1e-05)
    return centred * scale, scale


def norm_back(grad, unit, scale, gain):
    inner = grad * gain
    mean_one = jnp.mean(inner, axis=-1, keepdims=True)
    mean_two = jnp.mean(inner * unit, axis=-1, keepdims=True)
    return (inner - mean_one - unit * mean_two) * scale


def per_device(
    grid,
    passages,
    lengths,
    queries,
    positives,
    out_grad,
    w_query,
    b_query,
    w_key,
    w_value,
    b_value,
    w_out,
    b_out,
    norm1_gain,
    norm1_bias,
    w_up,
    b_up,
    w_down,
    b_down,
    norm2_gain,
    norm2_bias,
):
    steps, count, length, width = passages.shape
    head = width // H
    total = steps * count
    rows = total * length
    heads = (total, length, H, head)
    score_scale = 1.0 / math.sqrt(head)
    inv_width = 1.0 / math.sqrt(width)
    dp = grid.dp
    dp_index, rep_index = lax.axis_index("dp"), lax.axis_index("rep")
    here = jnp.stack([dp_index, rep_index]).astype(jnp.int32)

    block = w_query.shape[0]
    vectors = (b_query, b_value, b_out, norm1_gain, norm1_bias, b_down, norm2_gain, norm2_bias)
    spread = b_up.shape[0] // block
    columns = [v[:, None] for v in vectors] + [b_up.reshape(spread, block).T]
    columns = jnp.concatenate(columns, axis=1)
    columns = jnp.pad(columns, ((0, 0), (0, LANES - columns.shape[1])))
    if grid.fast:
        weight_q, weight_k, weight_v, table = gather_first(
            grid, here, (w_query, w_key, w_value), columns
        )
        weight_out, weight_up = gather_later(grid, here, (w_out, w_up))
        (weight_down,) = gather_later(grid, here, (w_down,))
    else:
        weight_q, weight_k, weight_v, table, weight_out, weight_up, weight_down = [
            lax.all_gather(w, "dp", axis=0, tiled=True)
            for w in (w_query, w_key, w_value, columns, w_out, w_up, w_down)
        ]
    table = table[:, :16].T.astype(F32)
    (bias_q, bias_v, bias_out, gain_one, shift_one, bias_down, gain_two, shift_two) = [
        table[i] for i in range(8)
    ]
    bias_up = jnp.transpose(
        table[8 : 8 + spread].reshape(spread, dp, block), (1, 0, 2)
    ).reshape(-1)
    digits = jnp.stack([positives.T // 256, positives.T % 256], axis=-1).astype(BF16)
    payload = jnp.concatenate(
        [
            jnp.moveaxis(queries, 0, 1),
            jnp.pad(digits, ((0, 0), (0, 0), (0, LANES - 2))),
        ],
        axis=-1,
    )
    payload = gather_small(grid, payload)
    all_queries = payload[:, :, :width]
    digits = payload[:, :, width : width + 2].astype(jnp.int32)
    all_positives = digits[:, :, 0] * 256 + digits[:, :, 1]

    tokens = passages.reshape(rows, width)
    key_valid = (jnp.arange(length)[None, :] < lengths.reshape(total)[:, None])[:, None, None, :]
    q = (mm(tokens, weight_q) + bias_q).astype(BF16).reshape(heads)
    k = mm(tokens, weight_k).astype(BF16).reshape(heads)
    v = (mm(tokens, weight_v) + bias_v).astype(BF16).reshape(heads)

    def scores_of():
        raw = jnp.einsum("plhe,pmhe->phlm", q, k, preferred_element_type=F32) * score_scale
        return jnp.where(key_valid, raw, -1000000000.0)

    scores = scores_of()
    log_total = jax.nn.logsumexp(scores, axis=-1, keepdims=True)
    probs_low = jnp.exp(scores - log_total).astype(BF16)
    context = jnp.einsum("phlm,pmhe->plhe", probs_low, v, preferred_element_type=F32)
    context = context.astype(BF16).reshape(rows, width)
    sum_one = tokens.astype(F32) + mm(context, weight_out) + bias_out
    unit_one, scale_one = norm_parts(sum_one)
    hidden = unit_one * gain_one + shift_one
    hidden_low = hidden.astype(BF16)
    pre = mm(hidden_low, weight_up) + bias_up
    phi, density = normal_parts(pre)
    gelu_low = (pre * phi).astype(BF16)
    slope = (phi + pre * density).astype(BF16)
    sum_two = hidden + mm(gelu_low, weight_down) + bias_down
    unit_two, scale_two = norm_parts(sum_two)
    result = (unit_two * gain_two + shift_two).reshape(steps, count, length, width)
    output = result.astype(BF16)

    all_cls = gather_small(grid, jnp.moveaxis(output[:, :, 0, :], 0, 1))
    first = (dp_index * grid.rep + rep_index) * count
    logits = jnp.einsum("qmd,pmd->mqp", all_queries, all_cls, preferred_element_type=F32)
    logits = logits * inv_width
    query_total = jax.nn.logsumexp(logits, axis=-1)
    passages_all = all_cls.shape[0]
    mine = lax.dynamic_slice_in_dim(logits, first, count, axis=1)
    mine_total = lax.dynamic_slice_in_dim(query_total, first, count, axis=1)
    onehot = (positives[:, :, None] == jnp.arange(passages_all)[None, None, :]).astype(F32)
    query_loss = mine_total - jnp.sum(mine * onehot, axis=-1)
    mine_grad = (jnp.exp(mine - mine_total[:, :, None]) - onehot) * inv_width
    queries_grad = jnp.einsum(
        "mqp,pmd->mqd", mine_grad.astype(BF16), all_cls, preferred_element_type=F32
    )
    column = lax.dynamic_slice_in_dim(logits, first, count, axis=2)
    hit = (all_positives.T[:, :, None] == (first + jnp.arange(count))[None, None, :]).astype(F32)
    column_grad = (jnp.exp(column - query_total[:, :, None]) - hit) * inv_width
    cls_grad = jnp.einsum(
        "mqp,qmd->mpd", column_grad.astype(BF16), all_queries, preferred_element_type=F32
    )

    grad_out = out_grad.astype(F32).at[:, :, 0, :].add(cls_grad).reshape(rows, width)
    grad_gain_two = jnp.sum(grad_out * unit_two, axis=0)
    grad_shift_two = jnp.sum(grad_out, axis=0)
    grad_two = norm_back(grad_out, unit_two, scale_two, gain_two)
    down_low = grad_two.astype(BF16)
    grad_b_down = row_total(down_low)
    shard_w_down = scatter_weight(grid, here, mm_left(gelu_low, down_low))
    up_low = (mm_back(down_low, weight_down) * slope.astype(F32)).astype(BF16)
    grad_b_up = row_total(up_low)
    shard_w_up = scatter_weight(grid, here, mm_left(hidden_low, up_low))
    grad_hidden = grad_two + mm_back(up_low, weight_up)
    grad_gain_one = jnp.sum(grad_hidden * unit_one, axis=0)
    grad_shift_one = jnp.sum(grad_hidden, axis=0)
    grad_one = norm_back(grad_hidden, unit_one, scale_one, gain_one)
    attn_low = grad_one.astype(BF16)
    grad_b_out = row_total(attn_low)
    shard_w_out = scatter_weight(grid, here, mm_left(context, attn_low))
    context_grad = mm_back(attn_low, weight_out).astype(BF16).reshape(heads)
    attn_probs = jnp.exp(scores_of() - log_total)
    probs_grad = jnp.einsum("plhe,pmhe->phlm", context_grad, v, preferred_element_type=F32)
    inner = jnp.sum(probs_grad * attn_probs, axis=-1, keepdims=True)
    score_low = (attn_probs * (probs_grad - inner)).astype(BF16)
    q_low = jnp.einsum("phlm,pmhe->plhe", score_low, k, preferred_element_type=F32) * score_scale
    q_low = q_low.astype(BF16).reshape(rows, width)
    k_low = jnp.einsum("phlm,plhe->pmhe", score_low, q, preferred_element_type=F32) * score_scale
    k_low = k_low.astype(BF16).reshape(rows, width)
    v_low = jnp.einsum("phlm,plhe->pmhe", probs_low, context_grad, preferred_element_type=F32)
    v_low = v_low.astype(BF16).reshape(rows, width)
    shard_w_query = scatter_weight(grid, here, mm_left(tokens, q_low))
    shard_w_key = scatter_weight(grid, here, mm_left(tokens, k_low))
    shard_w_value = scatter_weight(grid, here, mm_left(tokens, v_low))
    grad_b_query = row_total(q_low)
    grad_b_value = row_total(v_low)
    input_grad = (
        grad_one + mm_back(q_low, weight_q) + mm_back(k_low, weight_k) + mm_back(v_low, weight_v)
    )

    grads = (
        grad_b_query,
        grad_b_value,
        grad_b_out,
        grad_gain_one,
        grad_shift_one,
        grad_b_down,
        grad_gain_two,
        grad_shift_two,
    )
    grads = jnp.concatenate([jnp.stack(grads), grad_b_up.reshape(spread, width)])

    def mine_of(sums):
        low = lax.dynamic_slice_in_dim(sums[:8], dp_index * block, block, axis=1)
        return low, lax.dynamic_slice_in_dim(
            sums[8:].reshape(-1), dp_index * spread * block, spread * block, axis=0
        )

    low, s_b_up = scatter_small(grid, grads, mine_of)
    (s_b_q, s_b_v, s_b_out, s_gain1, s_shift1, s_b_down, s_gain2, s_shift2) = [
        low[i] for i in range(8)
    ]
    return (
        output,
        query_loss,
        input_grad.reshape(steps, count, length, width),
        queries_grad,
        cls_grad,
        shard_w_query,
        s_b_q,
        shard_w_key,
        shard_w_value,
        s_b_v,
        shard_w_out,
        s_b_out,
        s_gain1,
        s_shift1,
        shard_w_up,
        s_b_up,
        shard_w_down,
        s_b_down,
        s_gain2,
        s_shift2,
    )


def solution(mesh):
    both = ("dp", "rep")
    matrix, vector = P("dp", None), P("dp")
    weights = (
        matrix, vector, matrix, matrix, vector, matrix, vector, vector, vector,
        matrix, vector, matrix, vector, vector, vector,
    )
    grid = Grid(mesh.shape["dp"], mesh.shape["rep"], 768 // mesh.shape["dp"])
    wide = P(None, both, None, None)
    return jax.shard_map(
        functools.partial(per_device, grid),
        mesh=mesh,
        in_specs=(wide, P(None, both), P(None, both, None), P(None, both), wide) + weights,
        out_specs=(wide, P(None, both), wide, P(None, both, None), P(None, both, None)) + weights,
        check_vma=False,
    )
```

time: 661 us -> 561 us (0.85)
  starting transfers between devices: 253 us -> 66.5 us
  waiting for transfers between devices: 185 us -> 244 us
  matrix products: 136 us -> 99.3 us
  local copies, waits for them, and re-layouts: 35.3 us -> 70.5 us
  Pallas kernels: 0 us -> 20.1 us
  other arithmetic: 41.2 us -> 49.8 us
    ppermute x128 -> x139, starting transfers between devices: 253 us -> 66.5 us  [the longest x111 44.5 us: flip(): return lax.ppermute(value, 'dp', [(i, i ^ bit) for i in range(self.dp)])]
    ppermute x128 -> x139, waiting for transfers between devices: 185 us -> 244 us  [the longest x111 158 us: flip(): return lax.ppermute(value, 'dp', [(i, i ^ bit) for i in range(self.dp)])]
    unnamed x161 -> x392, local copies, waits for them, and re-layouts: 5.68 us -> 34 us
    dot_general x6, matrix products: 46.9 us -> 21.4 us  [mm(): return jnp.dot(left, right, preferred_element_type=F32)]
    pallas_call x0 -> x9, Pallas kernels: none -> 20.1 us  [the longest x6 10.5 us: split(): pl.pallas_call(functools.partial(split_kernel, keys=keys), out_shape=[jax...]
    concatenate x0 -> x18, other arithmetic: none -> 11 us  [the longest x6 2.86 us: scatter_weight(): jnp.concatenate([added(BF16, *x_low), added(BF16, *x_high, got_x_high)])]
    dot_general x6, matrix products: 31.2 us -> 23.9 us  [mm_left(): lax.dot_general(left, right, (((0,), (0,)), ((), ())), preferred_element_...]
    convert_element_type x50 -> x62, other arithmetic: 13.4 us -> 13.9 us  [the longest x54 9.48 us: added(): return total.astype(kind)]
  transfers between devices with their start and end apart: 128 -> 139, of which waited for: 53 -> 74; matrix products, arithmetic and copies ran while one was open for 18% -> 14% of each run, Pallas kernels for 0% -> 2%
where the time goes in v2:
time: 561 us; the launch traced here: 555 us
  waiting for transfers between devices  244 us (43%)
  matrix products  99.3 us (18%)
  local copies, waits for them, and re-layouts  70.5 us (13%)
  starting transfers between devices  66.5 us (12%)
  other arithmetic  49.8 us (9%)
  Pallas kernels  20.1 us (4%)
    ppermute x111, waiting for transfers between devices, flip(): return lax.ppermute(value, 'dp', [(i, i ^ bit) for i in range(self.dp)])  158 us
    ppermute x28, waiting for transfers between devices, flip(): return lax.ppermute(value, 'rep', [(i, i ^ 1) for i in range(self.rep)])  86.9 us
    ppermute x111, starting transfers between devices, flip(): return lax.ppermute(value, 'dp', [(i, i ^ bit) for i in range(self.dp)])  44.5 us
    dot_general x6, matrix products, mm_back(): lax.dot_general(left, right, (((1,), (1,)), ((), ())), preferred_element_...  35.6 us
    unnamed x392, local copies, waits for them, and re-layouts  34 us
    dot_general x6, matrix products, mm_left(): lax.dot_general(left, right, (((0,), (0,)), ((), ())), preferred_element_...  23.9 us
    ppermute x28, starting transfers between devices, flip(): return lax.ppermute(value, 'rep', [(i, i ^ 1) for i in range(self.rep)])  22 us
    dot_general x6, matrix products, mm(): return jnp.dot(left, right, preferred_element_type=F32)  21.4 us
  transfers between devices with their start and end apart: 139, of which 74 were waited for; matrix products, arithmetic and copies ran while one was open for 14% of the time, Pallas kernels for 2%

profile of v2, /device:TPU:0, one launch (start us, length us, event | category | flops | bytes accessed | tf_op | source)
XLA Modules:
  0.0 554.7 jit_solution(9026035950393091937)
XLA Ops:
  23.1 6.7 %collective-permute-done.4.refs_4_ = bf16[2,48,1280]{2,1,0:T(8,128)(2,1)S(1)} collective-permute-done((bf16[2,48,1280]{2,1,0:T(8,128)(2,1)S(1)}, bf16[2,48,1280]{2,1,0:T(8,128)(2,1)S(1)}, u32[]{:S(2)}, u32[]{:S(2)}) %collective-permute-start.4) | collective-permute-done | bytes 245792 | tf_op jit(solution)/shard_map/ppermute | solution.py:33
  46.9 23.0 %collective-permute-done.30 = bf16[2,192,384]{2,1,0:T(8,128)(2,1)} collective-permute-done((bf16[2,192,384]{2,1,0:T(8,128)(2,1)}, bf16[2,192,384]{2,1,0:T(8,128)(2,1)}, u32[]{:S(2)}, u32[]{:S(2)}) %collective-permute-start.30) | collective-permute-done | bytes 294944 | tf_op jit(solution)/shard_map/ppermute | solution.py:35
  103.2 5.5 collective-permute-done.20.refs_1_
  110.3 5.6 %collective-permute-done.33.refs_3_ = bf16[2,192,384]{2,1,0:T(8,128)(2,1)S(1)} collective-permute-done((bf16[2,192,384]{2,1,0:T(8,128)(2,1)S(1)}, bf16[2,192,384]{2,1,0:T(8,128)(2,1)S(1)}, u32[]{:S(2)}, u32[]{:S(2)}) %collective-permute-start.33) | collective-permute-done | bytes 294944 | tf_op jit(solution)/shard_map/ppermute | solution.py:33
  145.1 5.2 join.4
  152.9 9.6 %multiply_convert_fusion.1 = (bf16[1024,3072]{1,0:T(8,128)(2,1)S(1)}, f32[1024,3072]{1,0:T(8,128)}) fusion(f32[3072]{0:T(1024)S(1)} %add.457, bf16[768,3072]{1,0:T(8,128)(2,1)S(1)} %get-tuple-element.127, f32[1024,768]{1,0:T(8,128)S(1)} %get-tuple-element.289, f32[768]{0:T(1024)S(1)} %get-tuple-element.223, f32[768]{0:T(1024)S(1)} %get-tuple-element.224, ...), kind=kOutput, calls=%fused_computation.8 | convolution fusion | flops 4854644736 | bytes 26765312 | tf_op jit(solution)/shard_map/dot_general | solution.py:232
  162.6 5.5 fusion.126
  180.1 8.6 %collective-permute-done.44 = bf16[64,2,896]{2,0,1:T(8,128)(2,1)S(1)} collective-permute-done((bf16[64,2,896]{2,0,1:T(8,128)(2,1)S(1)}, bf16[64,2,896]{2,0,1:T(8,128)(2,1)S(1)}, u32[]{:S(2)}, u32[]{:S(2)}) %collective-permute-start.44) | collective-permute-done | bytes 229408 | tf_op jit(solution)/shard_map/ppermute | solution.py:35
  189.1 9.1 %collective-permute-done.49 = bf16[64,2,768]{2,0,1:T(8,128)(2,1)S(1)} collective-permute-done((bf16[64,2,768]{2,0,1:T(8,128)(2,1)S(1)}, bf16[64,2,768]{2,0,1:T(8,128)(2,1)S(1)}, u32[]{:S(2)}, u32[]{:S(2)}) %collective-permute-start.49) | collective-permute-done | bytes 196640 | tf_op jit(solution)/shard_map/ppermute | solution.py:35
  209.9 10.1 %convolution_convert_fusion.value_ref = bf16[3072,768]{1,0:T(8,128)(2,1)} fusion(bf16[1024,3072]{1,0:T(8,128)(2,1)} %copy-done.182, f32[1024,768]{1,0:T(8,128)S(1)} %get-tuple-element.229), kind=kOutput, calls=%fused_computation.15 | convolution fusion | flops 4834983936 | bytes 14155776 | tf_op jit(solution)/shard_map/dot_general | solution.py:236
  220.1 12.4 %convert_reduce_fusion = (f32[3072]{0:T(1024)}, bf16[1024,3072]{1,0:T(8,128)(2,1)S(1)}) fusion(f32[1024,3072]{1,0:T(8,128)} %get-tuple-element.291, f32[3072]{0:T(1024)S(1)} %copy-done.170, bf16[3072,768]{1,0:T(8,128)(2,1)S(1)} %bitcast.253, f32[1024,768]{1,0:T(8,128)S(1)} %get-tuple-element.229), kind=kOutput, calls=%fused_computation.6 | convolution fusion | flops 4879807488 | bytes 26763264 | tf_op jit(solution)/shard_map/dot_general | solution.py:240
  232.6 8.0 %convolution_convert_fusion.1.value_ref = bf16[768,3072]{1,0:T(8,128)(2,1)} fusion(bf16[1024,3072]{1,0:T(8,128)(2,1)S(1)} %get-tuple-element.306, f32[1024,768]{1,0:T(8,128)S(1)} %copy-done.128, f32[768]{0:T(1024)S(1)} %copy-done.174, f32[768]{0:T(1024)S(1)} %copy-done.166, f32[1024]{0:T(1024)S(1)} %copy-done.168, f32[1024]{0:T(1024)S(1)} %copy-done.164), kind=kOutput, calls=%fused_computation.16 | convolution fusion | flops 4838129664 | bytes 14170112 | tf_op jit(solution)/shard_map/dot_general | solution.py:236
  240.6 6.5 %multiply_reduce_fusion.1 = (f32[768]{0:T(1024)}, f32[1024]{0:T(1024)S(1)}, f32[1024]{0:T(1024)S(1)}, f32[768]{0:T(1024)}, f32[1024,768]{1,0:T(8,128)S(1)}) fusion(f32[1024,768]{1,0:T(8,128)S(1)} %copy-done.128, f32[1024]{0:T(1024)S(1)} %copy-done.168, f32[1024]{0:T(1024)S(1)} %copy-done.164, f32[768]{0:T(1024)S(1)} %copy-done.166, ...), kind=kOutput, calls=%fused_computation.23 | convolution fusion | flops 4839698432 | bytes 20472832 | tf_op jit(solution)/shard_map/dot_general | solution.py:240
  257.9 5.9 %convert_reduce_fusion.3 = (f32[12,64]{1,0:T(8,128)}, bf16[8,128,12,64]{1,3,2,0:T(8,128)(2,1)S(1)}) fusion(f32[8,12,128,128]{2,3,1,0:T(8,128)} %copy-done.124, f32[8,12,128]{2,1,0:T(8,128)S(1)} %copy-done.141, pred[8,128]{1,0:T(8,128)(4,1)S(1)} %copy-done.172, bf16[8,128,12,64]{1,0,3,2:T(8,128)(2,1)S(1)} %bitcast.271), kind=kOutput, calls=%fused_computation.25 | convolution fusion | flops 209976576 | bytes 9490432 | tf_op jit(solution)/shard_map/phlm,plhe->pmhe/dot_general | solution.py:413
  319.6 7.8 %add_add_fusion = f32[1024,768]{1,0:T(8,128)} fusion(f32[1024,768]{1,0:T(8,128)} %fusion.15, f32[1024,768]{1,0:T(8,128)} %copy-done.129, f32[1024,768]{1,0:T(8,128)} %fusion.19, bf16[768,768]{1,0:T(8,128)(2,1)} %copy-done.5, bf16[96,8,8,128]{3,2,1,0:T(8,128)(2,1)} %bitcast.263), kind=kOutput, calls=%fused_computation.27 | convolution fusion | flops 1210318848 | bytes 15335424 | tf_op jit(solution)/shard_map/dot_general | solution.py:240
  428.6 4.5 collective-permute-done.108
  433.8 6.3 %collective-permute-done.94 = bf16[2,48,384]{2,1,0:T(8,128)(2,1)S(1)} collective-permute-done((bf16[2,48,384]{2,1,0:T(8,128)(2,1)S(1)}, bf16[2,48,384]{2,1,0:T(8,128)(2,1)S(1)}, u32[]{:S(2)}, u32[]{:S(2)}) %collective-permute-start.94) | collective-permute-done | bytes 73760 | tf_op jit(solution)/shard_map/ppermute | solution.py:35
  440.1 6.3 %collective-permute-done.80 = bf16[2,48,384]{2,1,0:T(8,128)(2,1)S(1)} collective-permute-done((bf16[2,48,384]{2,1,0:T(8,128)(2,1)S(1)}, bf16[2,48,384]{2,1,0:T(8,128)(2,1)S(1)}, u32[]{:S(2)}, u32[]{:S(2)}) %collective-permute-start.80) | collective-permute-done | bytes 73760 | tf_op jit(solution)/shard_map/ppermute | solution.py:35
  446.4 5.2 collective-permute-done.61
  495.6 5.0 collective-permute-done.119
  503.8 10.3 %collective-permute-done.130 = bf16[4,192,384]{2,1,0:T(8,128)(2,1)S(1)} collective-permute-done((bf16[4,192,384]{2,1,0:T(8,128)(2,1)S(1)}, bf16[4,192,384]{2,1,0:T(8,128)(2,1)S(1)}, u32[]{:S(2)}, u32[]{:S(2)}) %collective-permute-start.130) | collective-permute-done | bytes 589856 | tf_op jit(solution)/shard_map/ppermute | solution.py:33
  517.6 8.8 %collective-permute-done.116 = bf16[4,48,1536]{2,1,0:T(8,128)(2,1)S(1)} collective-permute-done((bf16[4,48,1536]{2,1,0:T(8,128)(2,1)S(1)}, bf16[4,48,1536]{2,1,0:T(8,128)(2,1)S(1)}, u32[]{:S(2)}, u32[]{:S(2)}) %collective-permute-start.116) | collective-permute-done | bytes 589856 | tf_op jit(solution)/shard_map/ppermute | solution.py:33
  530.7 11.7 %collective-permute-done.122 = bf16[2,48,1536]{2,1,0:T(8,128)(2,1)S(1)} collective-permute-done((bf16[2,48,1536]{2,1,0:T(8,128)(2,1)S(1)}, bf16[2,48,1536]{2,1,0:T(8,128)(2,1)S(1)}, u32[]{:S(2)}, u32[]{:S(2)}) %collective-permute-start.122) | collective-permute-done | bytes 294944 | tf_op jit(solution)/shard_map/ppermute | solution.py:35
  543.6 4.7 collective-permute-done.123
  (889 shorter events, 358.3 us)
Async XLA Ops:
  9.8 30.3 %collective-permute-start = (bf16[2,48,1280]{2,1,0:T(8,128)(2,1)S(1)}, bf16[2,48,1280]{2,1,0:T(8,128)(2,1)S(1)}, u32[]{:S(2)}, u32[]{:S(2)}) collective-permute-start(bf16[2,48,1280]{2,1,0:T(8,128)(2,1)S(1)} %pad_maximum_fusion.13.refs_0_), channel_id=1, source_target_pairs={{0,4},{2,6},{4,0},{6,2},{8,12},{10,14},{12,8},{14,10},{16,20},{18,... | collective-permute-start | bytes 737288 | tf_op jit(solution)/shard_map/ppermute | solution.py:35
  11.4 31.3 %collective-permute-start.9 = (bf16[2,48,1280]{2,1,0:T(8,128)(2,1)S(1)}, bf16[2,48,1280]{2,1,0:T(8,128)(2,1)S(1)}, u32[]{:S(2)}, u32[]{:S(2)}) collective-permute-start(bf16[2,48,1280]{2,1,0:T(8,128)(2,1)S(1)} %pad_maximum_fusion.13.refs_0_), channel_id=1, source_target_pairs={{0,2},{2,0},{4,6},{6,4},{8,10},{10,8},{12,14},{14,12},{16,18},{18,... | collective-permute-start | bytes 737288 | tf_op jit(solution)/shard_map/ppermute | solution.py:35
  39.0 32.2 %collective-permute-start.19 = (bf16[2,48,1920]{2,1,0:T(8,128)(2,1)}, bf16[2,48,1920]{2,1,0:T(8,128)(2,1)}, u32[]{:S(2)}, u32[]{:S(2)}) collective-permute-start(bf16[2,48,1920]{2,1,0:T(8,128)(2,1)} %pad_maximum_fusion.7), channel_id=1, source_target_pairs={{0,16},{2,18},{4,20},{6,22},{8,24},{10,26},{12,28},{14,30},{16,0},... | collective-permute-start | bytes 1105928 | tf_op jit(solution)/shard_map/ppermute | solution.py:35
  40.1 29.8 %collective-permute-start.30 = (bf16[2,192,384]{2,1,0:T(8,128)(2,1)}, bf16[2,192,384]{2,1,0:T(8,128)(2,1)}, u32[]{:S(2)}, u32[]{:S(2)}) collective-permute-start(bf16[2,192,384]{2,1,0:T(8,128)(2,1)} %pad_maximum_fusion.8), channel_id=1, source_target_pairs={{0,16},{2,18},{4,20},{6,22},{8,24},{10,26},{12,28},{14,30},{16,0},... | collective-permute-start | bytes 884744 | tf_op jit(solution)/shard_map/ppermute | solution.py:35
  42.7 27.2 %collective-permute-start.10 = (bf16[2,48,1280]{2,1,0:T(8,128)(2,1)S(1)}, bf16[2,48,1280]{2,1,0:T(8,128)(2,1)S(1)}, u32[]{:S(2)}, u32[]{:S(2)}) collective-permute-start(bf16[2,48,1280]{2,1,0:T(8,128)(2,1)S(1)} %collective-permute-done.refs_1_), channel_id=1, source_target_pairs={{0,2},{2,0},{4,6},{6,4},{8,10},{10,8},{12,14},{14,12},{16,18},{18,... | collective-permute-start | bytes 737288 | tf_op jit(solution)/shard_map/ppermute | solution.py:35
  42.7 28.6 %collective-permute-start.7 = (bf16[2,48,1280]{2,1,0:T(8,128)(2,1)}, bf16[2,48,1280]{2,1,0:T(8,128)(2,1)S(1)}, u32[]{:S(2)}, u32[]{:S(2)}) collective-permute-start(bf16[2,48,1280]{2,1,0:T(8,128)(2,1)} %get-tuple-element.246), channel_id=1, source_target_pairs={{0,1},{1,0},{2,3},{3,2},{4,5},{5,4},{6,7},{7,6},{8,9},{9,8},{10,11... | collective-permute-start | bytes 737288 | tf_op jit(solution)/shard_map/ppermute | solution.py:33
  46.4 30.3 %collective-permute-start.12 = (bf16[2,48,1280]{2,1,0:T(8,128)(2,1)S(1)}, bf16[2,48,1280]{2,1,0:T(8,128)(2,1)S(1)}, u32[]{:S(2)}, u32[]{:S(2)}) collective-permute-start(bf16[2,48,1280]{2,1,0:T(8,128)(2,1)S(1)} %collective-permute-done.3.refs_3_), channel_id=1, source_target_pairs={{0,2},{2,0},{4,6},{6,4},{8,10},{10,8},{12,14},{14,12},{16,18},{18,... | collective-permute-start | bytes 737288 | tf_op jit(solution)/shard_map/ppermute | solution.py:35
  76.7 21.4 %collective-permute-start.31 = (bf16[4,192,384]{2,1,0:T(8,128)(2,1)S(1)}, bf16[4,192,384]{2,1,0:T(8,128)(2,1)S(1)}, u32[]{:S(2)}, u32[]{:S(2)}) collective-permute-start(bf16[4,192,384]{2,1,0:T(8,128)(2,1)S(1)} %pad_maximum_fusion.1.refs_0_), channel_id=1, source_target_pairs={{0,4},{2,6},{4,0},{6,2},{8,12},{10,14},{12,8},{14,10},{16,20},{18,... | collective-permute-start | bytes 1769480 | tf_op jit(solution)/shard_map/ppermute | solution.py:35
  78.3 23.2 %collective-permute-start.32 = (bf16[4,192,384]{2,1,0:T(8,128)(2,1)S(1)}, bf16[4,192,384]{2,1,0:T(8,128)(2,1)S(1)}, u32[]{:S(2)}, u32[]{:S(2)}) collective-permute-start(bf16[4,192,384]{2,1,0:T(8,128)(2,1)S(1)} %pad_maximum_fusion.1.refs_0_), channel_id=1, source_target_pairs={{0,1},{1,0},{2,3},{3,2},{4,5},{5,4},{6,7},{7,6},{8,9},{9,8},{10,11... | collective-permute-start | bytes 1769480 | tf_op jit(solution)/shard_map/ppermute | solution.py:33
  79.5 38.0 %collective-permute-start.35 = (bf16[4,192,384]{2,1,0:T(8,128)(2,1)S(1)}, bf16[4,192,384]{2,1,0:T(8,128)(2,1)S(1)}, u32[]{:S(2)}, u32[]{:S(2)}) collective-permute-start(bf16[4,192,384]{2,1,0:T(8,128)(2,1)S(1)} %pad_maximum_fusion.1.refs_0_), channel_id=1, source_target_pairs={{0,2},{2,0},{4,6},{6,4},{8,10},{10,8},{12,14},{14,12},{16,18},{18,... | collective-permute-start | bytes 1769480 | tf_op jit(solution)/shard_map/ppermute | solution.py:35
  79.6 29.2 %collective-permute-start.20 = (bf16[4,48,1920]{2,1,0:T(8,128)(2,1)S(1)}, bf16[4,48,1920]{2,1,0:T(8,128)(2,1)S(1)}, u32[]{:S(2)}, u32[]{:S(2)}) collective-permute-start(bf16[4,48,1920]{2,1,0:T(8,128)(2,1)S(1)} %pad_maximum_fusion.refs_0_), channel_id=1, source_target_pairs={{0,4},{2,6},{4,0},{6,2},{8,12},{10,14},{12,8},{14,10},{16,20},{18,... | collective-permute-start | bytes 2211848 | tf_op jit(solution)/shard_map/ppermute | solution.py:35
  80.2 30.1 %collective-permute-start.21 = (bf16[4,48,1920]{2,1,0:T(8,128)(2,1)S(1)}, bf16[4,48,1920]{2,1,0:T(8,128)(2,1)S(1)}, u32[]{:S(2)}, u32[]{:S(2)}) collective-permute-start(bf16[4,48,1920]{2,1,0:T(8,128)(2,1)S(1)} %pad_maximum_fusion.refs_0_), channel_id=1, source_target_pairs={{0,1},{1,0},{2,3},{3,2},{4,5},{5,4},{6,7},{7,6},{8,9},{9,8},{10,11... | collective-permute-start | bytes 2211848 | tf_op jit(solution)/shard_map/ppermute | solution.py:33
  295.7 105.4 %collective-permute-start.126 = (bf16[2,192,384]{2,1,0:T(8,128)(2,1)}, bf16[2,192,384]{2,1,0:T(8,128)(2,1)}, u32[]{:S(2)}, u32[]{:S(2)}) collective-permute-start(bf16[2,192,384]{2,1,0:T(8,128)(2,1)} %get-tuple-element.201), channel_id=1, source_target_pairs={{0,2},{2,0},{4,6},{6,4},{8,10},{10,8},{12,14},{14,12},{16,18},{18,... | collective-permute-start | bytes 884744 | tf_op jit(solution)/shard_map/ppermute | solution.py:35
  295.7 106.7 %collective-permute-start.128 = (bf16[2,192,384]{2,1,0:T(8,128)(2,1)}, bf16[2,192,384]{2,1,0:T(8,128)(2,1)}, u32[]{:S(2)}, u32[]{:S(2)}) collective-permute-start(bf16[2,192,384]{2,1,0:T(8,128)(2,1)} %get-tuple-element.205), channel_id=1, source_target_pairs={{0,2},{2,0},{4,6},{6,4},{8,10},{10,8},{12,14},{14,12},{16,18},{18,... | collective-permute-start | bytes 884744 | tf_op jit(solution)/shard_map/ppermute | solution.py:35
  301.1 32.7 %collective-permute-start.98 = (bf16[2,48,384]{2,1,0:T(8,128)(2,1)}, bf16[2,48,384]{2,1,0:T(8,128)(2,1)}, u32[]{:S(2)}, u32[]{:S(2)}) collective-permute-start(bf16[2,48,384]{2,1,0:T(8,128)(2,1)} %get-tuple-element.173), channel_id=1, source_target_pairs={{0,2},{2,0},{4,6},{6,4},{8,10},{10,8},{12,14},{14,12},{16,18},{18,... | collective-permute-start | bytes 221192 | tf_op jit(solution)/shard_map/ppermute | solution.py:35
  301.1 34.1 %collective-permute-start.100 = (bf16[2,48,384]{2,1,0:T(8,128)(2,1)}, bf16[2,48,384]{2,1,0:T(8,128)(2,1)}, u32[]{:S(2)}, u32[]{:S(2)}) collective-permute-start(bf16[2,48,384]{2,1,0:T(8,128)(2,1)} %get-tuple-element.177), channel_id=1, source_target_pairs={{0,2},{2,0},{4,6},{6,4},{8,10},{10,8},{12,14},{14,12},{16,18},{18,... | collective-permute-start | bytes 221192 | tf_op jit(solution)/shard_map/ppermute | solution.py:35
  354.8 131.8 %collective-permute-start.127 = (bf16[2,192,384]{2,1,0:T(8,128)(2,1)S(1)}, bf16[2,192,384]{2,1,0:T(8,128)(2,1)}, u32[]{:S(2)}, u32[]{:S(2)}) collective-permute-start(bf16[2,192,384]{2,1,0:T(8,128)(2,1)S(1)} %copy-done.100), channel_id=1, source_target_pairs={{0,2},{2,0},{4,6},{6,4},{8,10},{10,8},{12,14},{14,12},{16,18},{18,... | collective-permute-start | bytes 884744 | tf_op jit(solution)/shard_map/ppermute | solution.py:35
  382.4 26.0 %collective-permute-start.132 = (bf16[2,192,384]{2,1,0:T(8,128)(2,1)}, bf16[2,192,384]{2,1,0:T(8,128)(2,1)}, u32[]{:S(2)}, u32[]{:S(2)}) collective-permute-start(bf16[2,192,384]{2,1,0:T(8,128)(2,1)} %get-tuple-element.209), channel_id=1, source_target_pairs={{0,2},{2,0},{4,6},{6,4},{8,10},{10,8},{12,14},{14,12},{16,18},{18,... | collective-permute-start | bytes 884744 | tf_op jit(solution)/shard_map/ppermute | solution.py:35
  403.8 87.0 %collective-permute-start.131 = (bf16[2,192,384]{2,1,0:T(8,128)(2,1)S(1)}, bf16[2,192,384]{2,1,0:T(8,128)(2,1)S(1)}, u32[]{:S(2)}, u32[]{:S(2)}) collective-permute-start(bf16[2,192,384]{2,1,0:T(8,128)(2,1)S(1)} %copy-done.98), channel_id=1, source_target_pairs={{0,2},{2,0},{4,6},{6,4},{8,10},{10,8},{12,14},{14,12},{16,18},{18,... | collective-permute-start | bytes 884744 | tf_op jit(solution)/shard_map/ppermute | solution.py:35
  422.8 78.7 %collective-permute-start.125 = (bf16[4,192,384]{2,1,0:T(8,128)(2,1)S(1)}, bf16[4,192,384]{2,1,0:T(8,128)(2,1)S(1)}, u32[]{:S(2)}, u32[]{:S(2)}) collective-permute-start(bf16[4,192,384]{2,1,0:T(8,128)(2,1)S(1)} %copy-done.94), channel_id=1, source_target_pairs={{0,2},{2,0},{4,6},{6,4},{8,10},{10,8},{12,14},{14,12},{16,18},{18,... | collective-permute-start | bytes 1769480 | tf_op jit(solution)/shard_map/ppermute | solution.py:35
  425.4 55.4 %collective-permute-start.113 = (bf16[2,48,1536]{2,1,0:T(8,128)(2,1)S(1)}, bf16[2,48,1536]{2,1,0:T(8,128)(2,1)S(1)}, u32[]{:S(2)}, u32[]{:S(2)}) collective-permute-start(bf16[2,48,1536]{2,1,0:T(8,128)(2,1)S(1)} %copy-done.102), channel_id=1, source_target_pairs={{0,2},{2,0},{4,6},{6,4},{8,10},{10,8},{12,14},{14,12},{16,18},{18,... | collective-permute-start | bytes 884744 | tf_op jit(solution)/shard_map/ppermute | solution.py:35
  489.7 27.9 %collective-permute-start.111 = (bf16[4,48,1536]{2,1,0:T(8,128)(2,1)S(1)}, bf16[4,48,1536]{2,1,0:T(8,128)(2,1)S(1)}, u32[]{:S(2)}, u32[]{:S(2)}) collective-permute-start(bf16[4,48,1536]{2,1,0:T(8,128)(2,1)S(1)} %copy-done.92), channel_id=1, source_target_pairs={{0,2},{2,0},{4,6},{6,4},{8,10},{10,8},{12,14},{14,12},{16,18},{18,... | collective-permute-start | bytes 1769480 | tf_op jit(solution)/shard_map/ppermute | solution.py:35
  501.4 24.9 %collective-permute-start.116 = (bf16[4,48,1536]{2,1,0:T(8,128)(2,1)S(1)}, bf16[4,48,1536]{2,1,0:T(8,128)(2,1)S(1)}, u32[]{:S(2)}, u32[]{:S(2)}) collective-permute-start(bf16[4,48,1536]{2,1,0:T(8,128)(2,1)S(1)} %pad_maximum_fusion.2), channel_id=1, source_target_pairs={{0,1},{1,0},{2,3},{3,2},{4,5},{5,4},{6,7},{7,6},{8,9},{9,8},{10,11... | collective-permute-start | bytes 1769480 | tf_op jit(solution)/shard_map/ppermute | solution.py:33
  501.5 26.3 %collective-permute-start.121 = (bf16[4,48,1536]{2,1,0:T(8,128)(2,1)S(1)}, bf16[4,48,1536]{2,1,0:T(8,128)(2,1)S(1)}, u32[]{:S(2)}, u32[]{:S(2)}) collective-permute-start(bf16[4,48,1536]{2,1,0:T(8,128)(2,1)S(1)} %pad_maximum_fusion.3), channel_id=1, source_target_pairs={{0,4},{2,6},{4,0},{6,2},{8,12},{10,14},{12,8},{14,10},{16,20},{18,... | collective-permute-start | bytes 1769480 | tf_op jit(solution)/shard_map/ppermute | solution.py:35
  (308 other events, 3412.3 us)
